TPU v7x, 128 devices: a whole 4x4x4 slice. The times are simulated.
128 devices in a mesh: dp: 8 (over z_lo, y), ep: 16 (over x, z_hi, core).
Axes of the slice: x: 4, y: 4, z: 4 (z_hi: 2, z_lo: 2; z = z_hi * 2 + z_lo), core: 2. Of those that a mesh axis runs over, the one named last changes fastest.
Arguments:
- queries: bfloat16 [512, 36864], P('dp', 'ep'), may hold values from -60 to 60
- cache_latent: bfloat16 [512, 80, 512], P('dp'), may hold values from -6 to 6
- cache_rope: bfloat16 [512, 80, 64], P('dp'), may hold values from -6 to 6
- cache_len: int32 [512], P('dp'), may hold values from 1 to 80, as said below
- move_plan: int32 [512], replicated, may hold values from 0 to 511, as said below
- w_absorb: bfloat16 [64, 512, 128], P('ep'), may hold values from -0.25 to 0.25
- w_out: bfloat16 [8192, 7168], P('ep'), may hold values from -0.0625 to 0.0625
- norm_gain: float32 [7168], replicated, may hold values from 0.1 to 1.9
- router: bfloat16 [7168, 16], replicated, may hold values from -0.0625 to 0.0625
- routes: int32 [512, 8], P('dp'), may hold values from 0 to 15, all different within a row; in each aligned block of 64 rows (0 to 63, 64 to 127, ...) at most 40 rows name the same one
- w_gate: bfloat16 [16, 7168, 2048], P('ep', None, 'dp'), may hold values from -0.0625 to 0.0625
- w_up: bfloat16 [16, 7168, 2048], P('ep', None, 'dp'), may hold values from -0.0625 to 0.0625
- w_down: bfloat16 [16, 2048, 7168], P('ep', 'dp'), may hold values from -0.125 to 0.125
Outputs:
- attended: bfloat16 [512, 7168], P('dp')
- expert_mix: bfloat16 [512, 7168], P(('dp', 'ep'))
Inputs may be any that keep to these rules, and one draw needn't show every extreme that they name: `cache_len`: some request has all 80 positions filled and some only one. `move_plan`: A permutation of the slots. The dp ranks fall into two halves of 4 ranks; each rank of one half swaps exactly 2 requests with each rank of the other half; every other request keeps its slot. `routes`: in the 64 rows of one dp rank no expert is named by more than 40 rows, a bound that some block reaches.
All inputs are finite; a program needn't handle non-finite values.
Results may differ from a plain program's by a relative error of at most 0.035.
Values may be sent and summed in bfloat16 or wider, within the bound.
A program may use at most 128 MiB of HBM per device.

v0:
```python
import jax
import jax.numpy as jnp
from jax import lax
from jax.sharding import PartitionSpec as P

ROPE = 64
VDIM = 128
MIGP = 2


epsilon = 1e-06
route_scale = 2.5


def move_caches(cache_latent, cache_rope, cache_len, move_plan):
    rank_count = lax.axis_size("dp")
    slot_count = cache_len.shape[0]
    myself = lax.axis_index("dp")
    plan_table = move_plan.reshape(rank_count, slot_count)
    source_rank = plan_table // slot_count
    source_slot = plan_table % slot_count
    others = jnp.arange(rank_count, dtype=jnp.int32)[:, None] != myself
    outgoing = (source_rank == myself) & others
    mailbox = jnp.cumsum(outgoing.astype(jnp.int32), axis=1) - 1
    letters = jnp.arange(MIGP, dtype=jnp.int32)
    chosen = outgoing[:, :, None] & (mailbox[:, :, None] == letters[None, None, :])
    send_slot = jnp.sum(jnp.where(chosen, source_slot[:, :, None], 0), axis=1)
    packed = (
        cache_latent[send_slot],
        cache_rope[send_slot],
        cache_len[send_slot].astype(jnp.bfloat16),
    )
    got_latent, got_rope, got_length = (
        lax.all_to_all(packed[0], "dp", split_axis=0, concat_axis=0, tiled=True),
        lax.all_to_all(packed[1], "dp", split_axis=0, concat_axis=0, tiled=True),
        lax.all_to_all(packed[2], "dp", split_axis=0, concat_axis=0, tiled=True),
    )
    own_rank = lax.dynamic_index_in_dim(source_rank, myself, 0, keepdims=False)
    own_slot = lax.dynamic_index_in_dim(source_slot, myself, 0, keepdims=False)
    incoming = own_rank != myself
    position = jnp.arange(slot_count, dtype=jnp.int32)
    earlier = (own_rank[:, None] == own_rank[None, :]) & (position[None, :] < position[:, None])
    letter = jnp.sum(earlier.astype(jnp.int32), axis=1)
    pool_index = jnp.where(incoming, slot_count + own_rank * MIGP + letter, own_slot)
    latent_pool = jnp.concatenate(
        [cache_latent, got_latent.reshape((-1,) + cache_latent.shape[1:])], 0
    )
    rope_pool = jnp.concatenate([cache_rope, got_rope.reshape((-1,) + cache_rope.shape[1:])], 0)
    length_pool = jnp.concatenate([cache_len, got_length.reshape(-1).astype(jnp.int32)], 0)
    return (latent_pool[pool_index], rope_pool[pool_index], length_pool[pool_index])


def attend(queries, latent, rope_keys, lengths, w_absorb):
    slot_count = latent.shape[0]
    head_count = w_absorb.shape[0]
    latent_width = latent.shape[2]
    score_scale = (VDIM + ROPE) ** (-0.5)
    shaped = queries.reshape(slot_count, head_count, -1)
    scores = jnp.einsum(
        "shl,stl->sht", shaped[:, :, :latent_width], latent, preferred_element_type=jnp.float32
    )
    scores = scores + jnp.einsum(
        "shr,str->sht", shaped[:, :, latent_width:], rope_keys, preferred_element_type=jnp.float32
    )
    scores = scores * score_scale
    positions = jnp.arange(latent.shape[1], dtype=jnp.int32)
    scores = jnp.where(positions[None, None, :] < lengths[:, None, None], scores, -jnp.inf)
    scores = scores - jnp.max(scores, axis=2, keepdims=True)
    expsum = jnp.exp(scores)
    weights_soft = (expsum / jnp.sum(expsum, axis=2, keepdims=True)).astype(jnp.bfloat16)
    latent_out = jnp.einsum(
        "sht,stl->shl", weights_soft, latent, preferred_element_type=jnp.float32
    ).astype(jnp.bfloat16)
    values = jnp.einsum(
        "shl,hlv->shv", latent_out, w_absorb, preferred_element_type=jnp.float32
    ).astype(jnp.bfloat16)
    return values.reshape(slot_count, -1)


def per_device(
    queries,
    cache_latent,
    cache_rope,
    cache_len,
    move_plan,
    w_absorb,
    w_out,
    norm_gain,
    router,
    routes,
    w_gate,
    w_up,
    w_down,
):
    latent, rope_keys, lengths = move_caches(cache_latent, cache_rope, cache_len, move_plan)
    values = attend(queries, latent, rope_keys, lengths, w_absorb)
    head_terms = jnp.dot(values, w_out, preferred_element_type=jnp.float32)
    hidden_sum = lax.psum(head_terms.astype(jnp.bfloat16), "ep").astype(jnp.float32)
    attended = hidden_sum.astype(jnp.bfloat16)
    meansq = jnp.mean(hidden_sum * hidden_sum, axis=1, keepdims=True)
    normed = (hidden_sum * lax.rsqrt(meansq + epsilon) * norm_gain).astype(jnp.bfloat16)
    affinity = jax.nn.sigmoid(jnp.dot(normed, router, preferred_element_type=jnp.float32))
    chosen = jnp.take_along_axis(affinity, routes, axis=1)
    route_weight = route_scale * chosen / jnp.sum(chosen, axis=1, keepdims=True)
    expert_id = lax.axis_index("ep")
    weight_mine = jnp.sum(jnp.where(routes == expert_id, route_weight, 0.0), axis=1)
    gate_slice = w_gate[0]
    up_slice = w_up[0]
    down_slice = w_down[0]
    segment = lax.all_gather(normed, "dp", axis=0, tiled=True)
    gate_act = jnp.dot(segment, gate_slice, preferred_element_type=jnp.float32)
    up_act = jnp.dot(segment, up_slice, preferred_element_type=jnp.float32)
    hidden = (jax.nn.silu(gate_act) * up_act).astype(jnp.bfloat16)
    expert_out = lax.psum_scatter(
        jnp.dot(hidden, down_slice, preferred_element_type=jnp.float32).astype(jnp.bfloat16),
        "dp",
        scatter_dimension=0,
        tiled=True,
    ).astype(jnp.float32)
    contrib = weight_mine[:, None] * expert_out
    mixture = lax.psum_scatter(contrib.astype(jnp.bfloat16), "ep", scatter_dimension=0, tiled=True)
    return (attended, mixture)


def solution(mesh):
    in_specs = (
        P("dp", "ep"),
        P("dp", None, None),
        P("dp", None, None),
        P("dp"),
        P(),
        P("ep", None, None),
        P("ep", None),
        P(),
        P(),
        P("dp", None),
        P("ep", None, "dp"),
        P("ep", None, "dp"),
        P("ep", "dp", None),
    )
    out_specs = (P("dp", None), P(("dp", "ep"), None))
    return jax.shard_map(
        per_device, mesh=mesh, in_specs=in_specs, out_specs=out_specs, check_vma=False
    )
```

profile of v0, /device:TPU:1, one launch (start us, length us, event | category | flops | bytes accessed | tf_op | source)
XLA Modules:
  0.0 561.3 jit_solution(5264230706505995945)
XLA Ops:
  7.2 0.8 reshape.265
  8.1 0.2 reduce_window_sum.11
  8.3 0.1 select_reduce_fusion
  8.5 0.1 copy.47
  8.6 0.1 reshape.274
  8.7 1.4 gather_fusion
  10.0 0.7 convert_element_type.82
  10.7 6.4 %all-to-all-start = ((bf16[8,1,2]{2,1,0:T(2,128)(2,1)}), bf16[8,1,2]{2,1,0:T(2,128)(2,1)S(1)}, u32[]{:S(2)}, u32[]{:S(2)}) async-start(bf16[8,1,2]{2,1,0:T(2,128)(2,1)} %convert_element_type.82), calls=%async_computation | async-start | bytes 8192 | tf_op jit(solution)/shard_map/all_to_all | solution.py:36
  17.1 2.5 gather_fusion.4
  19.6 2.4 all-to-all-done
  22.0 3.4 all-to-all-start.2
  25.4 4.2 gather_fusion.2
  29.6 0.4 reshape.267
  30.0 1.5 all-to-all-done.2
  31.6 3.6 all-to-all-start.1
  35.2 0.2 convert_reduce_fusion
  35.6 0.8 gather_fusion.1
  36.5 2.6 pad_maximum_fusion.1
  39.0 2.1 gather_fusion.5
  41.1 12.6 %all-to-all-done.1 = bf16[8,2,80,512]{3,2,1,0:T(8,128)(2,1)S(1)} async-done(((bf16[8,2,80,512]{3,2,1,0:T(8,128)(2,1)}), bf16[8,2,80,512]{3,2,1,0:T(8,128)(2,1)S(1)}, u32[]{:S(2)}, u32[]{:S(2)}) %all-to-all-start.1) | async-done | bytes 1310752 | tf_op jit(solution)/shard_map/all_to_all | solution.py:34
  53.7 5.8 %pad_maximum_fusion = bf16[80,80,512]{2,1,0:T(8,128)(2,1)} fusion(bf16[16,80,512]{2,1,0:T(8,128)(2,1)S(1)} %bitcast.71, bf16[64,80,512]{2,1,0:T(8,128)(2,1)} %param.14), kind=kLoop, calls=%fused_computation.10 | loop fusion | flops 3276800 | bytes 13107200 | tf_op jit(solution)/shard_map/concatenate | solution.py:45
  59.5 6.1 %gather_fusion.3 = bf16[64,80,512]{2,1,0:T(8,128)(2,1)} fusion(bf16[80,80,512]{2,1,0:T(8,128)(2,1)} %pad_maximum_fusion, s32[1024]{0:T(1024)S(1)} %pad_clamp_fusion), kind=kCustom, calls=%fused_computation.3 | custom fusion | bytes 10486016 | tf_op jit(solution)/shard_map/gather | solution.py:50
  65.6 3.9 fusion.26
  69.6 0.4 fusion.19
  70.0 0.2 fusion.43
  70.2 3.5 convolution_convert_fusion.2
  73.7 0.2 fusion.20
  74.0 5.4 convolution_convert_fusion.1
  79.5 139.9 %all-reduce.4.cloned.1.call-done = bf16[64,7168]{1,0:T(8,128)(2,1)} async-done(((bf16[64,7168]{1,0:T(8,128)(2,1)}), bf16[64,7168]{1,0:T(8,128)(2,1)}) %all-reduce.4.cloned.1.call-update) | async-done | bytes 917520 | tf_op jit(solution)/shard_map/psum | solution.py:98
  219.4 1.5 fusion.6
  220.9 2.4 fusion.8
  223.3 0.2 reduce-scatter.2.cloned.1.call-start
  223.5 83.1 %all-gather.2.cloned.1.call-done = bf16[512,7168]{1,0:T(8,128)(2,1)} async-done(((bf16[64,7168]{1,0:T(8,128)(2,1)}), bf16[512,7168]{1,0:T(8,128)(2,1)}) %all-gather.2.cloned.1.call-update) | async-done | bytes 7340048 | tf_op jit(solution)/shard_map/all_gather | solution.py:110
  306.6 6.2 %fusion.4 = f32[512,256]{1,0:T(8,128)S(1)} fusion(bf16[512,7168]{1,0:T(8,128)(2,1)} %all-gather.2.cloned.1.call-done, bf16[1,7168,256]{2,1,0:T(8,128)(2,1)} %param.23), kind=kOutput, calls=%fused_computation.14 | convolution fusion | flops 1879048192 | bytes 11534336 | tf_op jit(solution)/shard_map/dot_general | solution.py:111
  312.8 16.0 %convolution_convert_fusion = bf16[512,7168]{1,0:T(8,128)(2,1)} fusion(bf16[1,256,7168]{2,1,0:T(8,128)(2,1)} %param.25, bf16[512,7168]{1,0:T(8,128)(2,1)} %all-gather.2.cloned.1.call-done, bf16[1,7168,256]{2,1,0:T(8,128)(2,1)} %param.24, f32[512,256]{1,0:T(8,128)S(1)} %fusion.4), kind=kOutput, calls=%fused_computation.8 | convolution fusion | flops 3762552832 | bytes 22544384 | tf_op jit(solution)/shard_map/dot_general | solution.py:115
  328.8 0.6 copy-done.6
  329.4 0.1 copy.51
  329.5 0.1 reshape.320
  329.6 0.3 copy-done.3
  330.0 0.3 fusion.23
  330.3 3.9 gather_fusion.6
  334.2 0.1 reshape.323
  334.4 76.1 %reduce-scatter.2.cloned.1.call-done = bf16[64,7168]{1,0:T(8,128)(2,1)} async-done(((bf16[512,7168]{1,0:T(8,128)(2,1)}), bf16[64,7168]{1,0:T(8,128)(2,1)}) %reduce-scatter.2.cloned.1.call-update) | async-done | bytes 917520 | tf_op jit(solution)/shard_map/reduce_scatter | solution.py:114
  410.5 2.3 multiply_convert_fusion
  412.9 0.6 dynamic-slice
  414.1 138.1 %all-reduce.6.cloned.1.call-done = bf16[64,7168]{1,0:T(8,128)(2,1)} async-done(((bf16[64,7168]{1,0:T(8,128)(2,1)}), bf16[64,7168]{1,0:T(8,128)(2,1)}) %all-reduce.6.cloned.1.call-update) | async-done | bytes 917520
  552.3 1.6 constant_dynamic-slice_fusion
  553.8 0.9 copy.62
  (41 shorter events, 0.8 us)
Async XLA Ops:
  7.2 66.6 %copy-start = (bf16[4,512,128]{2,1,0:T(8,128)(2,1)S(1)}, bf16[4,512,128]{2,1,0:T(8,128)(2,1)}, u32[]{:S(2)}) copy-start(bf16[4,512,128]{2,1,0:T(8,128)(2,1)} %param.18) | copy-start | bytes 1572868
  8.7 21.0 %copy-start.4 = (bf16[64,2304]{1,0:T(8,128)(2,1)S(1)}, bf16[64,2304]{1,0:T(8,128)(2,1)}, u32[]{:S(2)}) copy-start(bf16[64,2304]{1,0:T(8,128)(2,1)} %param.13) | copy-start | bytes 884740
  10.0 25.5 %copy-start.1 = (s32[64]{0:T(128)S(1)}, s32[64]{0:T(128)}, u32[]{:S(2)}) copy-start(s32[64]{0:T(128)} %param.16) | copy-start | bytes 772
  10.7 11.3 %all-to-all-start = ((bf16[8,1,2]{2,1,0:T(2,128)(2,1)}), bf16[8,1,2]{2,1,0:T(2,128)(2,1)S(1)}, u32[]{:S(2)}, u32[]{:S(2)}) async-start(bf16[8,1,2]{2,1,0:T(2,128)(2,1)} %convert_element_type.82), calls=%async_computation | async-start | bytes 8192 | tf_op jit(solution)/shard_map/all_to_all | solution.py:36
  22.0 9.5 %all-to-all-start.2 = ((bf16[8,2,80,64]{2,3,1,0:T(8,128)(2,1)}), bf16[8,2,80,64]{2,3,1,0:T(8,128)(2,1)S(1)}, u32[]{:S(2)}, u32[]{:S(2)}) async-start(bf16[8,2,80,64]{2,3,1,0:T(8,128)(2,1)} %bitcast.9), calls=%async_computation.2 | async-start | bytes 524288 | tf_op jit(solution)/shard_map/all_to_all | solution.py:35
  31.6 22.2 %all-to-all-start.1 = ((bf16[8,2,80,512]{3,2,1,0:T(8,128)(2,1)}), bf16[8,2,80,512]{3,2,1,0:T(8,128)(2,1)S(1)}, u32[]{:S(2)}, u32[]{:S(2)}) async-start(bf16[8,2,80,512]{3,2,1,0:T(8,128)(2,1)} %bitcast.72), calls=%async_computation.1 | async-start | bytes 2621440 | tf_op jit(solution)/shard_map/all_to_all | solution.py:34
  35.1 184.2 %all-reduce.4.cloned.1.call-start = ((), (), s32[]{:S(2)}) async-start(), calls=%async_computation.4 | async-start | bytes 1835008 | tf_op jit(solution)/shard_map/psum | solution.py:98
  74.0 146.9 %copy-start.7 = (f32[7168]{0:T(1024)S(1)}, f32[7168]{0:T(1024)}, u32[]{:S(2)}) copy-start(f32[7168]{0:T(1024)} %param.20) | copy-start | bytes 86020
  79.5 227.1 %all-gather.2.cloned.1.call-start = ((), (), s32[]{:S(2)}) async-start(), calls=%async_computation.5 | async-start | bytes 8257536 | tf_op jit(solution)/shard_map/all_gather | solution.py:110
  223.3 187.3 %reduce-scatter.2.cloned.1.call-start = ((), (), s32[]{:S(2)}) async-start(), calls=%async_computation.6 | async-start | bytes 8257536 | tf_op jit(solution)/shard_map/reduce_scatter | solution.py:114
  328.7 0.7 copy-start.6
  328.7 1.2 copy-start.3
  328.7 1.2 copy-start.5
  328.8 223.5 %all-reduce.6.cloned.1.call-start = ((), (), s32[]{:S(2)}) async-start(), calls=%async_computation.7 | async-start | bytes 1835008
  330.3 82.6 %copy-start.8 = (u32[128]{0:T(128)S(1)}, u32[128]{0:T(128)}, u32[]{:S(2)}) copy-start(u32[128]{0:T(128)} %constant.111) | copy-start | bytes 1540
  330.3 223.5 %copy-start.2 = (bf16[64,7168]{1,0:T(8,128)(2,1)S(1)}, bf16[64,7168]{1,0:T(8,128)(2,1)}, u32[]{:S(2)}) copy-start(bf16[64,7168]{1,0:T(8,128)(2,1)} %all-reduce.4.cloned.1.call-done) | copy-start | bytes 2752516
Sparse Core Ops, SparseCore 0:
  79.6 139.7 all-reduce.3
  223.4 83.1 all-gather.1
  328.9 81.5 reduce-scatter.1
  413.6 138.6 all-reduce.5
where the time goes:
time: 562 us; the launch traced here: 561 us
  waiting for transfers between devices  454 us (81%)
  matrix products  36 us (6%)
  local copies, waits for them, and re-layouts  27.4 us (5%)
  other arithmetic  15.6 us (3%)
  between operations  14.6 us (3%)
  starting transfers between devices  13.7 us (2%)
    psum x1, waiting for transfers between devices, per_device(): lax.psum(head_terms.astype(jnp.bfloat16), 'ep').astype(jnp.float32)  140 us
    unnamed x5, waiting for transfers between devices  138 us
    all_gather x1, waiting for transfers between devices, per_device(): segment = lax.all_gather(normed, 'dp', axis=0, tiled=True)  83.1 us
    reduce_scatter x1, waiting for transfers between devices, per_device(): lax.psum_scatter(jnp.dot(hidden, down_slice, preferred_element_type=jnp.f...  76.1 us
    dot_general x1, matrix products, per_device(): jnp.dot(hidden, down_slice, preferred_element_type=jnp.float32)  16 us
    all_to_all x1, waiting for transfers between devices, move_caches(): lax.all_to_all(packed[0], 'dp', split_axis=0, concat_axis=0, tiled=True)  12.6 us
  transfers between devices with their start and end apart: 7, of which 7 were waited for; matrix products, arithmetic and copies ran while one was open for 3% of the time, Pallas kernels for 0%

commit v1 on v0

--- a/solution.py
+++ b/solution.py
@@ -1,6 +1,8 @@
 import jax
 import jax.numpy as jnp
 from jax import lax
+from jax.experimental import pallas as pl
+from jax.experimental.pallas import tpu as pltpu
 from jax.sharding import PartitionSpec as P
 
 ROPE = 64
@@ -77,6 +79,446 @@
     return values.reshape(slot_count, -1)
 
 
+MESH = pl.DeviceIdType.MESH
+AXES = ("x", "z", "y")
+ORDERS = (("y", "z", "x"), ("z", "x", "y"), ("x", "y", "z"))
+
+
+def coordinates():
+    dp, ep = lax.axis_index("dp"), lax.axis_index("ep")
+    me = {"x": ep // 4, "z": (ep // 2) % 2 * 2 + dp // 4, "y": dp % 4}
+    return me, ep % 2
+
+
+def device(at, core):
+    return ((at["z"] % 2) * 4 + at["y"], at["x"] * 4 + at["z"] // 2 * 2 + core)
+
+
+def moved(me, axis, offset):
+    return {**me, axis: (me[axis] + offset) % 4}
+
+
+def pick(ref, where, tail=(), axes=AXES):
+    return ref.at[tuple(where.get(a, slice(None)) for a in axes) + tuple(tail)]
+
+
+class Copies:
+    def __init__(self, send, recv):
+        self.send, self.recv, self.used, self.sent = send, recv, 0, []
+
+    def start(self, src, dst, to):
+        copy = pltpu.make_async_remote_copy(
+            src_ref=src,
+            dst_ref=dst,
+            send_sem=self.send.at[self.used],
+            recv_sem=self.recv.at[self.used],
+            device_id=to,
+            device_id_type=MESH,
+        )
+        copy.start()
+        self.used += 1
+        self.sent.append(copy)
+        return copy
+
+    def finish(self):
+        for copy in self.sent:
+            copy.wait_send()
+
+
+def experts_kernel(
+    values,
+    routes,
+    gain,
+    w_out,
+    router,
+    w_gate,
+    w_up,
+    w_down,
+    attended,
+    mixed,
+    wo,
+    wr,
+    wg,
+    wu,
+    wd,
+    terms,
+    core_terms,
+    slab_terms,
+    tokens,
+    gate_sum,
+    up_sum,
+    score_sum,
+    square_sum,
+    act,
+    partial,
+    core_partial,
+    far_parts,
+    near_parts,
+    sums_two,
+    parts_two,
+    sums_three,
+    parts_three,
+    final_half,
+    load_sem,
+    send_sem,
+    recv_sem,
+):
+    me, core = coordinates()
+    other = 1 - core
+    sibling = device(me, other)
+    copies = Copies(send_sem, recv_sem)
+    width = wg.shape[1]
+    slots = values.shape[0]
+    half = slots // 2
+    tiles = width // 128
+    wide = (tiles * 5 + 6) // 7 * 128
+    piece_rows = ((0, half // 2), (half // 2, half // 2), (0, half))
+    piece_cols = ((0, wide), (0, wide), (wide, width - wide))
+    unit_cols = partial.shape[-1]
+    share = (unit_cols // 128 * 5 + 6) // 14 * 128
+    out_cols = ((0, share), (share, share), (2 * share, unit_cols - 2 * share))
+
+    slab_offsets = [(dx, dz) for dx in range(4) for dz in range(2) if (dx, dz) != (0, 0)]
+
+    def slab_chip(dx, dz):
+        return {**me, "x": (me["x"] + dx) % 4, "z": (me["z"] + 2 * dz) % 4}
+
+    def slab_index(chip):
+        return chip["x"] * 2 + chip["z"] // 2
+
+    order = slab_offsets + [(0, 0)]
+    slabs = [slab_index(slab_chip(dx, dz)) for dx, dz in order]
+
+    def columns(slab):
+        return pl.ds(pl.multiple_of(slab * width, 128), width)
+
+    loads = []
+    for k, slab in enumerate(slabs):
+        loads.append(
+            pltpu.make_async_copy(w_out.at[:, columns(slab)], wo.at[:, columns(slab)], load_sem.at[k])
+        )
+    for k, (source, target) in enumerate(((w_gate, wg), (w_up, wu), (router, wr), (w_down, wd))):
+        loads.append(pltpu.make_async_copy(source, target, load_sem.at[8 + k]))
+    for load in loads:
+        load.start()
+
+    peers = [sibling]
+    for axis in AXES:
+        peers += [device(moved(me, axis, k), core) for k in (1, 2, 3)]
+    peers += [device(slab_chip(dx, 1), core) for dx in (1, 2, 3)]
+    barrier = pltpu.get_barrier_semaphore()
+    for peer in peers:
+        pl.semaphore_signal(barrier, inc=1, device_id=peer, device_id_type=MESH)
+    pl.semaphore_wait(barrier, len(peers))
+
+    from_sibling = []
+    for k, slab in enumerate(slabs):
+        loads[k].wait()
+        head_terms = jnp.dot(values[...], wo[:, columns(slab)], preferred_element_type=jnp.float32)
+        terms[k] = head_terms.astype(jnp.bfloat16).reshape(2, half, width)
+        from_sibling.append(copies.start(terms.at[k, other], core_terms.at[k], sibling))
+    from_slabs = []
+    for k, (dx, dz) in enumerate(order):
+        from_sibling[k].wait_recv()
+        total = terms[k, core].astype(jnp.float32) + core_terms[k].astype(jnp.float32)
+        if k < len(slab_offsets):
+            terms[k, core] = total.astype(jnp.bfloat16)
+            from_slabs.append(
+                copies.start(terms.at[k, core], slab_terms.at[k], device(slab_chip(dx, dz), core))
+            )
+    for k, copy in enumerate(from_slabs):
+        copy.wait_recv()
+        total = total + slab_terms[k].astype(jnp.float32)
+    own_rows = pl.ds(pl.multiple_of(core * half, 16), half)
+    tokens[me["x"], me["z"], me["y"], own_rows, :] = total.astype(jnp.bfloat16)
+
+    def block(p, where):
+        first, count = piece_rows[p]
+        rows = pl.ds(pl.multiple_of(core * half + first, 16), count)
+        return pick(tokens, where, (rows, pl.ds(*piece_cols[p])))
+
+    def spread(p, where, to):
+        return copies.start(block(p, where), block(p, where), to)
+
+    to_core = []
+    phase_one, phase_two = {}, {}
+    for p, (first, second, last) in enumerate(ORDERS):
+        phase_one[p] = [spread(p, me, device(moved(me, first, k), core)) for k in (1, 3, 2)]
+    for p, (first, second, last) in enumerate(ORDERS):
+        for copy in phase_one[p]:
+            copy.wait_recv()
+        where = {second: me[second], last: me[last]}
+        phase_two[p] = [spread(p, where, device(moved(me, second, k), core)) for k in (1, 3, 2)]
+    near = {}
+    for p, (first, second, last) in enumerate(ORDERS):
+        for copy in phase_two[p]:
+            copy.wait_recv()
+        parts = [{last: me[last], second: pl.ds(0, 2)}, {last: me[last], second: pl.ds(2, 2)}]
+        right, left = device(moved(me, last, 1), core), device(moved(me, last, 3), core)
+        right_a, left_b = spread(p, parts[0], right), spread(p, parts[1], left)
+        right_b, left_a = spread(p, parts[1], right), spread(p, parts[0], left)
+        near[p] = (right_a, right_b, left_a, left_b)
+        to_core.append(spread(p, {last: me[last]}, sibling))
+    far = {}
+    for p, (first, second, last) in enumerate(ORDERS):
+        right_a, right_b, left_a, left_b = near[p]
+        right, left = device(moved(me, last, 1), core), device(moved(me, last, 3), core)
+        before, after = (me[last] + 3) % 4, (me[last] + 1) % 4
+        right_a.wait_recv()
+        forward_a = spread(p, {last: before, second: pl.ds(0, 2)}, right)
+        left_b.wait_recv()
+        forward_b = spread(p, {last: after, second: pl.ds(2, 2)}, left)
+        far[p] = (forward_a, forward_b)
+    for p, (first, second, last) in enumerate(ORDERS):
+        right_a, right_b, left_a, left_b = near[p]
+        before, after = (me[last] + 3) % 4, (me[last] + 1) % 4
+        right_b.wait_recv()
+        to_core.append(spread(p, {last: before}, sibling))
+        left_a.wait_recv()
+        to_core.append(spread(p, {last: after}, sibling))
+    for p, (first, second, last) in enumerate(ORDERS):
+        for copy in far[p]:
+            copy.wait_recv()
+        to_core.append(spread(p, {last: (me[last] + 2) % 4}, sibling))
+    for copy in to_core:
+        copy.wait_recv()
+
+    rank_copies = []
+    for slab in range(8):
+        rank_copies.append(
+            pltpu.make_async_copy(
+                tokens.at[slab // 2, slab % 2 * 2 + me["z"] % 2, me["y"]],
+                attended.at[:, pl.ds(slab * width, width)],
+                load_sem.at[12 + slab],
+            )
+        )
+        rank_copies[-1].start()
+
+    for load in loads[8:]:
+        load.wait()
+    gate_sum[...] = jnp.zeros_like(gate_sum)
+    up_sum[...] = jnp.zeros_like(up_sum)
+    score_sum[...] = jnp.zeros_like(score_sum)
+    square_sum[...] = jnp.zeros_like(square_sum)
+
+    @pl.loop(0, 8)
+    def _(slab):
+        rows = tokens[slab // 2, pl.ds(slab % 2 * 2, 2)].reshape(8 * slots, width).astype(jnp.float32)
+        square_sum[...] += jnp.sum(rows * rows, axis=1, keepdims=True)
+        gained = (rows * gain[slab]).astype(jnp.bfloat16)
+        gate_sum[...] += jnp.dot(gained, wg[slab], preferred_element_type=jnp.float32)
+        up_sum[...] += jnp.dot(gained, wu[slab], preferred_element_type=jnp.float32)
+        score_sum[...] += jnp.dot(gained, wr[slab], preferred_element_type=jnp.float32)
+
+    scale = lax.rsqrt(square_sum[...] * (1.0 / (8 * width)) + epsilon)
+    scores = score_sum[...] * scale
+    affinity = 1.0 / (1.0 + jnp.exp(-scores))
+    experts = lax.broadcasted_iota(jnp.int32, scores.shape, 1)
+    named = jnp.zeros(scores.shape, jnp.float32)
+    for k in range(routes.shape[1]):
+        named = named + jnp.where(routes[:, k : k + 1] == experts, 1.0, 0.0)
+    chosen = affinity * named
+    mine = jnp.sum(jnp.where(experts == lax.axis_index("ep"), chosen, 0.0), axis=1, keepdims=True)
+    weight = route_scale * mine / jnp.sum(chosen, axis=1, keepdims=True)
+    gate = gate_sum[...] * scale
+    hidden = gate / (1.0 + jnp.exp(-gate)) * (up_sum[...] * scale) * weight
+    act[...] = hidden.astype(jnp.bfloat16)
+
+    def down(p, column_half):
+        first, count = out_cols[p]
+        quarters = []
+        for quarter in range(2):
+            start = pl.multiple_of(column_half * (2 * unit_cols) + quarter * unit_cols + first, 128)
+            quarters.append(
+                jnp.dot(act[...], wd[:, pl.ds(start, count)], preferred_element_type=jnp.float32)
+                .reshape(2, 4, 4, 2, 8, count)
+            )
+        both = jnp.concatenate(quarters, axis=4).astype(jnp.bfloat16)
+        for zl in range(2):
+            for y in range(4):
+                for zh in range(2):
+                    partial[column_half, :, zh * 2 + zl, y, :, pl.ds(first, count)] = both[zl, y, :, zh]
+
+    units = range(3)
+    to_core = []
+    for p in units:
+        down(p, other)
+        cols = pl.ds(*out_cols[p])
+        to_core.append(
+            copies.start(partial.at[other, :, :, :, :, cols], core_partial.at[:, :, :, :, cols], sibling)
+        )
+    rest = [tuple(a for a in AXES if a != order[2]) for order in ORDERS]
+    far, near = {}, {}
+
+    for p, (first, second, last) in enumerate(ORDERS):
+        cols = pl.ds(*out_cols[p])
+        width_p = out_cols[p][1]
+        down(p, core)
+        to_core[p].wait_recv()
+
+        @pl.loop(0, 4)
+        def _(x):
+            partial[core, x, :, :, :, cols] = (
+                partial[core, x, :, :, :, cols].astype(jnp.float32)
+                + core_partial[x, :, :, :, cols].astype(jnp.float32)
+            ).astype(jnp.bfloat16)
+
+        def source(where):
+            return pick(partial.at[core], where, (slice(None), cols))
+
+        right, left = device(moved(me, last, 1), core), device(moved(me, last, 3), core)
+        before, after, across = (me[last] + 3) % 4, (me[last] + 1) % 4, (me[last] + 2) % 4
+        tail = (slice(None), pl.ds(0, width_p))
+
+        def landing(ref, where):
+            return pick(ref, where, tail, rest[p])
+
+        a, b = {second: pl.ds(0, 2)}, {second: pl.ds(2, 2)}
+        far_a = copies.start(source({last: across, **a}), landing(far_parts.at[p], a), right)
+        far_b = copies.start(source({last: across, **b}), landing(far_parts.at[p], b), left)
+        right_b = copies.start(source({last: after, **b}), landing(near_parts.at[p, 0], b), right)
+        left_a = copies.start(source({last: before, **a}), landing(near_parts.at[p, 1], a), left)
+        far[p], near[p] = (far_a, far_b), [right_b, left_a]
+
+    for p, (first, second, last) in enumerate(ORDERS):
+        cols = pl.ds(*out_cols[p])
+        width_p = out_cols[p][1]
+        right, left = device(moved(me, last, 1), core), device(moved(me, last, 3), core)
+        before, after = (me[last] + 3) % 4, (me[last] + 1) % 4
+        tail = (slice(None), pl.ds(0, width_p))
+        for side, (copy, part, at, to) in enumerate(
+            ((far[p][0], pl.ds(0, 2), after, right), (far[p][1], pl.ds(2, 2), before, left))
+        ):
+            copy.wait_recv()
+            here = pick(partial.at[core], {last: at, second: part}, (slice(None), cols))
+            came = pick(far_parts.at[p], {second: part}, tail, rest[p])
+            here[...] = (here[...].astype(jnp.float32) + came[...].astype(jnp.float32)).astype(jnp.bfloat16)
+            near[p].append(copies.start(here, pick(near_parts.at[p, side], {second: part}, tail, rest[p]), to))
+
+    phase_two = {}
+    for p, (first, second, last) in enumerate(ORDERS):
+        cols = pl.ds(*out_cols[p])
+        width_p = out_cols[p][1]
+        tail = (slice(None), pl.ds(0, width_p))
+        for copy in near[p]:
+            copy.wait_recv()
+        here = pick(partial.at[core], {last: me[last]}, (slice(None), cols))
+        total = here[...].astype(jnp.float32)
+        for side in range(2):
+            total = total + near_parts[p, side, :, :, :, pl.ds(0, width_p)].astype(jnp.float32)
+        sums_two[p, :, :, :, pl.ds(0, width_p)] = total.astype(jnp.bfloat16)
+        phase_two[p] = []
+        for k in (1, 3, 2):
+            to = moved(me, second, k)
+            phase_two[p].append(
+                copies.start(
+                    pick(sums_two.at[p], {second: to[second]}, tail, rest[p]),
+                    parts_two.at[p, k - 1, :, :, pl.ds(0, width_p)],
+                    device(to, core),
+                )
+            )
+    phase_three = {}
+    for p, (first, second, last) in enumerate(ORDERS):
+        width_p = out_cols[p][1]
+        tail = (slice(None), pl.ds(0, width_p))
+        for copy in phase_two[p]:
+            copy.wait_recv()
+        total = pick(sums_two.at[p], {second: me[second]}, tail, rest[p])[...].astype(jnp.float32)
+        for k in range(3):
+            total = total + parts_two[p, k, :, :, pl.ds(0, width_p)].astype(jnp.float32)
+        sums_three[p, :, :, pl.ds(0, width_p)] = total.astype(jnp.bfloat16)
+        phase_three[p] = []
+        for k in (1, 3, 2):
+            to = moved(me, first, k)
+            phase_three[p].append(
+                copies.start(
+                    sums_three.at[p, to[first], :, pl.ds(0, width_p)],
+                    parts_three.at[p, k - 1, :, pl.ds(0, width_p)],
+                    device(to, core),
+                )
+            )
+    for p, (first, second, last) in enumerate(ORDERS):
+        width_p = out_cols[p][1]
+        for copy in phase_three[p]:
+            copy.wait_recv()
+        total = sums_three[p, me[first], :, pl.ds(0, width_p)].astype(jnp.float32)
+        for k in range(3):
+            total = total + parts_three[p, k, :, pl.ds(0, width_p)].astype(jnp.float32)
+        final_half[0, :, pl.ds(*out_cols[p])] = total.astype(jnp.bfloat16)
+    last_copy = copies.start(final_half.at[0], final_half.at[1], sibling)
+    mixed[core] = final_half[0]
+    last_copy.wait_recv()
+    mixed[other] = final_half[1]
+    for copy in rank_copies:
+        copy.wait()
+    copies.finish()
+
+
+def run_experts(values, routes, gain, w_out, router, w_gate, w_up, w_down):
+    slots, heads_width = values.shape
+    model = w_out.shape[1]
+    width = model // 8
+    half = slots // 2
+    hidden = w_gate.shape[1]
+    experts = router.shape[1]
+    rows = 8 * slots
+    unit_cols = model // 4
+    share = (unit_cols // 128 * 5 + 6) // 14 * 128
+    bf16, f32 = jnp.bfloat16, jnp.float32
+    vmem = pl.BlockSpec(memory_space=pltpu.VMEM)
+    hbm = pl.BlockSpec(memory_space=pl.ANY)
+    return pl.pallas_call(
+        experts_kernel,
+        out_shape=(
+            jax.ShapeDtypeStruct((slots, model), bf16),
+            jax.ShapeDtypeStruct((2, 16, unit_cols), bf16),
+        ),
+        in_specs=[vmem, vmem, vmem, hbm, hbm, hbm, hbm, hbm],
+        out_specs=(hbm, vmem),
+        scratch_shapes=[
+            pltpu.VMEM((heads_width, model), bf16),
+            pltpu.VMEM((8, width, experts), bf16),
+            pltpu.VMEM((8, width, hidden), bf16),
+            pltpu.VMEM((8, width, hidden), bf16),
+            pltpu.VMEM((hidden, model), bf16),
+            pltpu.VMEM((8, 2, half, width), bf16),
+            pltpu.VMEM((8, half, width), bf16),
+            pltpu.VMEM((7, half, width), bf16),
+            pltpu.VMEM((4, 4, 4, slots, width), bf16),
+            pltpu.VMEM((rows, hidden), f32),
+            pltpu.VMEM((rows, hidden), f32),
+            pltpu.VMEM((rows, experts), f32),
+            pltpu.VMEM((rows, 1), f32),
+            pltpu.VMEM((rows, hidden), bf16),
+            pltpu.VMEM((2, 4, 4, 4, 16, unit_cols), bf16),
+            pltpu.VMEM((4, 4, 4, 16, unit_cols), bf16),
+            pltpu.VMEM((3, 4, 4, 16, share), bf16),
+            pltpu.VMEM((3, 2, 4, 4, 16, share), bf16),
+            pltpu.VMEM((3, 4, 4, 16, share), bf16),
+            pltpu.VMEM((3, 3, 4, 16, share), bf16),
+            pltpu.VMEM((3, 4, 16, share), bf16),
+            pltpu.VMEM((3, 3, 16, share), bf16),
+            pltpu.VMEM((2, 16, unit_cols), bf16),
+            pltpu.SemaphoreType.DMA((20,)),
+            pltpu.SemaphoreType.DMA((112,)),
+            pltpu.SemaphoreType.DMA((112,)),
+        ],
+        compiler_params=pltpu.CompilerParams(
+            collective_id=0, has_side_effects=True, vmem_limit_bytes=60 * 1024 * 1024
+        ),
+        name="experts",
+    )(
+        values,
+        routes,
+        gain.reshape(8, 1, width),
+        w_out,
+        router.reshape(8, width, experts),
+        w_gate.reshape(8, width, hidden),
+        w_up.reshape(8, width, hidden),
+        w_down,
+    )
+
+
 def per_device(
     queries,
     cache_latent,
@@ -92,33 +534,16 @@
     w_up,
     w_down,
 ):
+    all_routes = lax.all_gather(routes, "dp", axis=0, tiled=True)
     latent, rope_keys, lengths = move_caches(cache_latent, cache_rope, cache_len, move_plan)
     values = attend(queries, latent, rope_keys, lengths, w_absorb)
-    head_terms = jnp.dot(values, w_out, preferred_element_type=jnp.float32)
-    hidden_sum = lax.psum(head_terms.astype(jnp.bfloat16), "ep").astype(jnp.float32)
-    attended = hidden_sum.astype(jnp.bfloat16)
-    meansq = jnp.mean(hidden_sum * hidden_sum, axis=1, keepdims=True)
-    normed = (hidden_sum * lax.rsqrt(meansq + epsilon) * norm_gain).astype(jnp.bfloat16)
-    affinity = jax.nn.sigmoid(jnp.dot(normed, router, preferred_element_type=jnp.float32))
-    chosen = jnp.take_along_axis(affinity, routes, axis=1)
-    route_weight = route_scale * chosen / jnp.sum(chosen, axis=1, keepdims=True)
-    expert_id = lax.axis_index("ep")
-    weight_mine = jnp.sum(jnp.where(routes == expert_id, route_weight, 0.0), axis=1)
-    gate_slice = w_gate[0]
-    up_slice = w_up[0]
-    down_slice = w_down[0]
-    segment = lax.all_gather(normed, "dp", axis=0, tiled=True)
-    gate_act = jnp.dot(segment, gate_slice, preferred_element_type=jnp.float32)
-    up_act = jnp.dot(segment, up_slice, preferred_element_type=jnp.float32)
-    hidden = (jax.nn.silu(gate_act) * up_act).astype(jnp.bfloat16)
-    expert_out = lax.psum_scatter(
-        jnp.dot(hidden, down_slice, preferred_element_type=jnp.float32).astype(jnp.bfloat16),
-        "dp",
-        scatter_dimension=0,
-        tiled=True,
-    ).astype(jnp.float32)
-    contrib = weight_mine[:, None] * expert_out
-    mixture = lax.psum_scatter(contrib.astype(jnp.bfloat16), "ep", scatter_dimension=0, tiled=True)
+    attended, mixed = run_experts(
+        values, all_routes, norm_gain, w_out, router, w_gate[0], w_up[0], w_down[0]
+    )
+    core = lax.axis_index("ep") % 2
+    quarters = mixed.reshape(2, 2, 2, 4, mixed.shape[-1])
+    own = lax.dynamic_index_in_dim(quarters, core, 2, keepdims=False)
+    mixture = own.transpose(2, 0, 1, 3).reshape(4, -1)
     return (attended, mixture)
 
 

time: 562 us -> 182 us (0.32)
  waiting for transfers between devices: 454 us -> 9.5 us
  Pallas kernels: 0 us -> 92.4 us
  matrix products: 36 us -> 8.1 us
  blocking collectives: 0 us -> 22.2 us
  between operations: 14.6 us -> 0.82 us
  other arithmetic: 15.6 us -> 8.19 us
    psum x1 -> x0, waiting for transfers between devices: 140 us -> none  [per_device(): lax.psum(head_terms.astype(jnp.bfloat16), 'ep').astype(jnp.float32)]
    unnamed x5 -> x0, waiting for transfers between devices: 138 us -> none
    pallas_call x0 -> x1, Pallas kernels: none -> 92.4 us  [run_experts(): pl.pallas_call(experts_kernel, out_shape=(jax.ShapeDtypeStruct((slots, mo...]
    all_gather x1 -> x0, waiting for transfers between devices: 83.1 us -> none  [per_device(): segment = lax.all_gather(normed, 'dp', axis=0, tiled=True)]
    reduce_scatter x1 -> x0, waiting for transfers between devices: 76.1 us -> none  [per_device(): lax.psum_scatter(jnp.dot(hidden, down_slice, preferred_element_type=jnp.f...]
    dot_general x4 -> x0, matrix products: 27.9 us -> none  [the longest x1 16 us: per_device(): jnp.dot(hidden, down_slice, preferred_element_type=jnp.float32)]
    all_gather x0 -> x1, blocking collectives: none -> 22.2 us  [per_device(): all_routes = lax.all_gather(routes, 'dp', axis=0, tiled=True)]
  transfers between devices with their start and end apart: 7 -> 3, of which waited for: 7 -> 2; matrix products, arithmetic and copies ran while one was open for 3% -> 8% of each run, Pallas kernels for 0% -> 0%
where the time goes in v1:
time: 182 us; the launch traced here: 181 us
  Pallas kernels  92.4 us (51%)
  local copies, waits for them, and re-layouts  26.1 us (14%)
  blocking collectives  22.2 us (12%)
  starting transfers between devices  14.1 us (8%)
  waiting for transfers between devices  9.5 us (5%)
  other arithmetic  8.19 us (4%)
  matrix products  8.1 us (4%)
    pallas_call x1, Pallas kernels, run_experts(): pl.pallas_call(experts_kernel, out_shape=(jax.ShapeDtypeStruct((slots, mo...  92.4 us
    all_gather x1, blocking collectives, per_device(): all_routes = lax.all_gather(routes, 'dp', axis=0, tiled=True)  22.2 us
    all_to_all x1, waiting for transfers between devices, move_caches(): lax.all_to_all(packed[0], 'dp', split_axis=0, concat_axis=0, tiled=True)  7.07 us
    all_to_all x1, starting transfers between devices, move_caches(): lax.all_to_all(packed[2], 'dp', split_axis=0, concat_axis=0, tiled=True)  6.37 us
    gather x1, local copies, waits for them, and re-layouts, move_caches(): latent_pool[pool_index]  6.12 us
    concatenate x1, other arithmetic, move_caches(): jnp.concatenate([cache_latent, got_latent.reshape((-1,) + cache_latent.sh...  5.78 us
    all_to_all x1, starting transfers between devices, move_caches(): lax.all_to_all(packed[0], 'dp', split_axis=0, concat_axis=0, tiled=True)  4.28 us
    gather x1, local copies, waits for them, and re-layouts, move_caches(): cache_latent[send_slot]  4.18 us
  transfers between devices with their start and end apart: 3, of which 2 were waited for; matrix products, arithmetic and copies ran while one was open for 8% of the time, Pallas kernels for 0%

profile of v1, /device:TPU:1, one launch (start us, length us, event | category | flops | bytes accessed | tf_op | source)
XLA Modules:
  0.0 181.3 jit_solution(12136226197586804604)
XLA Ops:
  0.6 0.0 copy-start
  0.6 0.0 copy-start.3
  0.7 0.0 copy-start.4
  0.7 0.8 reshape.257
  1.5 0.1 fusion.19
  1.6 0.2 reduce_window_sum.11
  1.8 0.1 select_reduce_fusion
  2.0 0.1 copy.31
  2.1 0.1 reshape.269
  2.2 0.0 copy-start.5
  2.2 1.3 gather_fusion
  3.5 0.0 copy-start.2
  3.5 0.7 convert_element_type.53
  4.2 6.4 %all-to-all-start = ((bf16[8,1,2]{2,1,0:T(2,128)(2,1)}), bf16[8,1,2]{2,1,0:T(2,128)(2,1)S(1)}, u32[]{:S(2)}, u32[]{:S(2)}) async-start(bf16[8,1,2]{2,1,0:T(2,128)(2,1)} %convert_element_type.53), calls=%async_computation | async-start | bytes 8192 | tf_op jit(solution)/shard_map/all_to_all | solution.py:38
  10.6 2.5 %gather_fusion.4 = bf16[16,80,64]{1,2,0:T(8,128)(2,1)} fusion(bf16[64,80,64]{1,2,0:T(8,128)(2,1)} %param.15, s32[1024]{0:T(1024)S(1)} %pad_clamp_fusion.1), kind=kCustom, calls=%fused_computation.4 | custom fusion | bytes 327744 | tf_op jit(solution)/shard_map/gather | solution.py:32
  13.1 2.4 %all-to-all-done = bf16[8,1,2]{2,1,0:T(2,128)(2,1)S(1)} async-done(((bf16[8,1,2]{2,1,0:T(2,128)(2,1)}), bf16[8,1,2]{2,1,0:T(2,128)(2,1)S(1)}, u32[]{:S(2)}, u32[]{:S(2)}) %all-to-all-start) | async-done | bytes 64 | tf_op jit(solution)/shard_map/all_to_all | solution.py:38
  15.5 3.4 %all-to-all-start.2 = ((bf16[8,2,80,64]{2,3,1,0:T(8,128)(2,1)}), bf16[8,2,80,64]{2,3,1,0:T(8,128)(2,1)S(1)}, u32[]{:S(2)}, u32[]{:S(2)}) async-start(bf16[8,2,80,64]{2,3,1,0:T(8,128)(2,1)} %bitcast.9), calls=%async_computation.2 | async-start | bytes 524288 | tf_op jit(solution)/shard_map/all_to_all | solution.py:37
  18.9 4.2 %gather_fusion.2 = bf16[16,80,512]{2,1,0:T(8,128)(2,1)} fusion(bf16[64,80,512]{2,1,0:T(8,128)(2,1)} %param.14, s32[1024]{0:T(1024)S(1)} %pad_clamp_fusion.1), kind=kCustom, calls=%fused_computation.2 | custom fusion | bytes 2621504 | tf_op jit(solution)/shard_map/gather | solution.py:31
  23.1 0.0 copy-done.3
  23.1 0.4 reshape.259
  23.5 0.0 copy-done.4
  23.5 1.7 copy.36
  25.2 0.0 copy-done.5
  25.2 22.2 %all-gather = s32[8,64,8]{1,2,0:T(8,128)S(1)} all-gather(s32[1,64,8]{1,2,0:T(8,128)S(1)} %bitcast.70), channel_id=1, replica_groups=mesh['dp'=8,'ep'=16] {'dp'}, dimensions={0}, use_global_device_ids=true | all-gather | bytes 18432 | tf_op jit(solution)/shard_map/all_gather | solution.py:537
  47.4 0.8 copy.35
  48.2 0.0 all-to-all-done.2
  48.2 4.3 %all-to-all-start.1 = ((bf16[8,2,80,512]{3,2,1,0:T(8,128)(2,1)}), bf16[8,2,80,512]{3,2,1,0:T(8,128)(2,1)S(1)}, u32[]{:S(2)}, u32[]{:S(2)}) async-start(bf16[8,2,80,512]{3,2,1,0:T(8,128)(2,1)} %bitcast.7), calls=%async_computation.1 | async-start | bytes 2621440 | tf_op jit(solution)/shard_map/all_to_all | solution.py:36
  52.5 0.2 convert_reduce_fusion
  52.8 0.1 reshape.266
  52.8 0.0 copy-done.1
  52.8 0.1 pad_add_fusion
  52.9 0.8 gather_fusion.1
  53.7 0.1 iota_compare_fusion.1
  53.8 1.3 pad_maximum_fusion.1
  55.1 2.1 %gather_fusion.5 = bf16[64,80,64]{1,2,0:T(8,128)(2,1)S(1)} fusion(bf16[80,80,64]{1,2,0:T(8,128)(2,1)} %pad_maximum_fusion.1, s32[1024]{0:T(1024)S(1)} %pad_clamp_fusion), kind=kCustom, calls=%fused_computation.5 | custom fusion | bytes 1310976 | tf_op jit(solution)/shard_map/gather | solution.py:52
  57.2 7.1 %all-to-all-done.1 = bf16[8,2,80,512]{3,2,1,0:T(8,128)(2,1)S(1)} async-done(((bf16[8,2,80,512]{3,2,1,0:T(8,128)(2,1)}), bf16[8,2,80,512]{3,2,1,0:T(8,128)(2,1)S(1)}, u32[]{:S(2)}, u32[]{:S(2)}) %all-to-all-start.1) | async-done | bytes 1310752 | tf_op jit(solution)/shard_map/all_to_all | solution.py:36
  64.3 5.8 %pad_maximum_fusion = bf16[80,80,512]{2,1,0:T(8,128)(2,1)} fusion(bf16[16,80,512]{2,1,0:T(8,128)(2,1)S(1)} %bitcast.61, bf16[64,80,512]{2,1,0:T(8,128)(2,1)} %param.14), kind=kLoop, calls=%fused_computation.7 | loop fusion | flops 3276800 | bytes 13107200 | tf_op jit(solution)/shard_map/concatenate | solution.py:47
  70.1 6.1 %gather_fusion.3 = bf16[64,80,512]{2,1,0:T(8,128)(2,1)} fusion(bf16[80,80,512]{2,1,0:T(8,128)(2,1)} %pad_maximum_fusion, s32[1024]{0:T(1024)S(1)} %pad_clamp_fusion), kind=kCustom, calls=%fused_computation.3 | custom fusion | bytes 10486016 | tf_op jit(solution)/shard_map/gather | solution.py:52
  76.2 3.9 %fusion.7 = f32[64,80,4]{1,2,0:T(4,128)S(1)} fusion(bf16[64,80,512]{2,1,0:T(8,128)(2,1)} %gather_fusion.3, bf16[64,4,576]{2,1,0:T(4,128)(2,1)S(1)} %reshape.259), kind=kOutput, calls=%fused_computation.18 | convolution fusion | flops 20971520 | bytes 5586944 | tf_op jit(solution)/shard_map/shl,stl->sht/dot_general | solution.py:61
  80.1 0.4 fusion.5
  80.5 0.2 fusion.20
  80.8 3.5 %convolution_convert_fusion = bf16[64,4,512]{2,1,0:T(4,128)(2,1)S(1)} fusion(bf16[64,80,512]{2,1,0:T(8,128)(2,1)} %gather_fusion.3, f32[64,4]{1,0:T(8,128)S(1)} %fusion.20, f32[64,4,80]{2,1,0:T(4,128)S(1)} %fusion.5), kind=kOutput, calls=%fused_computation.9 | convolution fusion | flops 21164368 | bytes 5587968 | tf_op jit(solution)/shard_map/sht,stl->shl/dot_general | solution.py:73
  84.3 0.2 fusion.6
  84.5 0.6 copy.43
  85.2 92.4 %experts.1 = (bf16[64,7168]{1,0:T(8,128)(2,1)}, bf16[2,16,1792]{2,1,0:T(8,128)(2,1)}) custom-call(bf16[64,512]{1,0:T(8,128)(2,1)} %bitcast.67, s32[512,8]{1,0:T(8,128)} %bitcast.65, f32[8,1,896]{2,1,0:T(1,128)} %bitcast.69, bf16[512,7168]{1,0:T(8,128)(2,1)} %w_out.1, bf16[8,896,16]{2,1,0:T(8,128)(2,1)} %bitcast.60, bf16[8,896,256]{2,1,0:T(8,128)(2,1)} %bitcast.62, ...), custom_call_target="tpu_custom_call" | custom-call | tf_op jit(solution)/shard_map/experts/pallas_call | solution.py:470
  177.5 0.9 reshape.264
  178.5 0.7 constant_dynamic-slice_fusion
  179.1 2.2 %copy.45 = bf16[64,7168]{1,0:T(8,128)(2,1)} copy(bf16[64,7168]{1,0:T(8,128)(2,1)} %get-tuple-element.13) | data formatting | bytes 1835008
  (12 shorter events, 0.1 us)
Async XLA Ops:
  0.6 83.7 %copy-start = (bf16[4,512,128]{2,1,0:T(8,128)(2,1)S(1)}, bf16[4,512,128]{2,1,0:T(8,128)(2,1)}, u32[]{:S(2)}) copy-start(bf16[4,512,128]{2,1,0:T(8,128)(2,1)} %param.18) | copy-start | bytes 1572868
  0.6 22.5 %copy-start.3 = (bf16[64,2304]{1,0:T(8,128)(2,1)S(1)}, bf16[64,2304]{1,0:T(8,128)(2,1)}, u32[]{:S(2)}) copy-start(bf16[64,2304]{1,0:T(8,128)(2,1)} %param.13) | copy-start | bytes 884740
  0.7 22.9 %copy-start.4 = (bf16[7168,16]{0,1:T(8,128)(2,1)S(1)}, bf16[7168,16]{0,1:T(8,128)(2,1)}, u32[]{:S(2)}) copy-start(bf16[7168,16]{0,1:T(8,128)(2,1)} %param.21) | copy-start | bytes 688132
  2.2 23.1 %copy-start.5 = (s32[64,8]{0,1:T(8,128)S(1)}, s32[64,8]{0,1:T(8,128)}, u32[]{:S(2)}) copy-start(s32[64,8]{0,1:T(8,128)} %param.22) | copy-start | bytes 6148
  3.5 49.4 %copy-start.1 = (s32[64]{0:T(128)S(1)}, s32[64]{0:T(128)}, u32[]{:S(2)}) copy-start(s32[64]{0:T(128)} %param.16) | copy-start | bytes 772
  3.5 50.3 %copy-start.2 = (bf16[64,80,64]{1,2,0:T(8,128)(2,1)S(1)}, bf16[64,80,64]{1,2,0:T(8,128)(2,1)}, u32[]{:S(2)}) copy-start(bf16[64,80,64]{1,2,0:T(8,128)(2,1)} %param.15) | copy-start | bytes 1966084
  4.2 11.3 %all-to-all-start = ((bf16[8,1,2]{2,1,0:T(2,128)(2,1)}), bf16[8,1,2]{2,1,0:T(2,128)(2,1)S(1)}, u32[]{:S(2)}, u32[]{:S(2)}) async-start(bf16[8,1,2]{2,1,0:T(2,128)(2,1)} %convert_element_type.53), calls=%async_computation | async-start | bytes 8192 | tf_op jit(solution)/shard_map/all_to_all | solution.py:38
  15.5 32.7 %all-to-all-start.2 = ((bf16[8,2,80,64]{2,3,1,0:T(8,128)(2,1)}), bf16[8,2,80,64]{2,3,1,0:T(8,128)(2,1)S(1)}, u32[]{:S(2)}, u32[]{:S(2)}) async-start(bf16[8,2,80,64]{2,3,1,0:T(8,128)(2,1)} %bitcast.9), calls=%async_computation.2 | async-start | bytes 524288 | tf_op jit(solution)/shard_map/all_to_all | solution.py:37
  48.2 16.0 %all-to-all-start.1 = ((bf16[8,2,80,512]{3,2,1,0:T(8,128)(2,1)}), bf16[8,2,80,512]{3,2,1,0:T(8,128)(2,1)S(1)}, u32[]{:S(2)}, u32[]{:S(2)}) async-start(bf16[8,2,80,512]{3,2,1,0:T(8,128)(2,1)} %bitcast.7), calls=%async_computation.1 | async-start | bytes 2621440 | tf_op jit(solution)/shard_map/all_to_all | solution.py:36

commit v2 on v1

--- a/solution.py
+++ b/solution.py
@@ -5,78 +5,10 @@
 from jax.experimental.pallas import tpu as pltpu
 from jax.sharding import PartitionSpec as P
 
-ROPE = 64
 VDIM = 128
-MIGP = 2
-
 
 epsilon = 1e-06
 route_scale = 2.5
-
-
-def move_caches(cache_latent, cache_rope, cache_len, move_plan):
-    rank_count = lax.axis_size("dp")
-    slot_count = cache_len.shape[0]
-    myself = lax.axis_index("dp")
-    plan_table = move_plan.reshape(rank_count, slot_count)
-    source_rank = plan_table // slot_count
-    source_slot = plan_table % slot_count
-    others = jnp.arange(rank_count, dtype=jnp.int32)[:, None] != myself
-    outgoing = (source_rank == myself) & others
-    mailbox = jnp.cumsum(outgoing.astype(jnp.int32), axis=1) - 1
-    letters = jnp.arange(MIGP, dtype=jnp.int32)
-    chosen = outgoing[:, :, None] & (mailbox[:, :, None] == letters[None, None, :])
-    send_slot = jnp.sum(jnp.where(chosen, source_slot[:, :, None], 0), axis=1)
-    packed = (
-        cache_latent[send_slot],
-        cache_rope[send_slot],
-        cache_len[send_slot].astype(jnp.bfloat16),
-    )
-    got_latent, got_rope, got_length = (
-        lax.all_to_all(packed[0], "dp", split_axis=0, concat_axis=0, tiled=True),
-        lax.all_to_all(packed[1], "dp", split_axis=0, concat_axis=0, tiled=True),
-        lax.all_to_all(packed[2], "dp", split_axis=0, concat_axis=0, tiled=True),
-    )
-    own_rank = lax.dynamic_index_in_dim(source_rank, myself, 0, keepdims=False)
-    own_slot = lax.dynamic_index_in_dim(source_slot, myself, 0, keepdims=False)
-    incoming = own_rank != myself
-    position = jnp.arange(slot_count, dtype=jnp.int32)
-    earlier = (own_rank[:, None] == own_rank[None, :]) & (position[None, :] < position[:, None])
-    letter = jnp.sum(earlier.astype(jnp.int32), axis=1)
-    pool_index = jnp.where(incoming, slot_count + own_rank * MIGP + letter, own_slot)
-    latent_pool = jnp.concatenate(
-        [cache_latent, got_latent.reshape((-1,) + cache_latent.shape[1:])], 0
-    )
-    rope_pool = jnp.concatenate([cache_rope, got_rope.reshape((-1,) + cache_rope.shape[1:])], 0)
-    length_pool = jnp.concatenate([cache_len, got_length.reshape(-1).astype(jnp.int32)], 0)
-    return (latent_pool[pool_index], rope_pool[pool_index], length_pool[pool_index])
-
-
-def attend(queries, latent, rope_keys, lengths, w_absorb):
-    slot_count = latent.shape[0]
-    head_count = w_absorb.shape[0]
-    latent_width = latent.shape[2]
-    score_scale = (VDIM + ROPE) ** (-0.5)
-    shaped = queries.reshape(slot_count, head_count, -1)
-    scores = jnp.einsum(
-        "shl,stl->sht", shaped[:, :, :latent_width], latent, preferred_element_type=jnp.float32
-    )
-    scores = scores + jnp.einsum(
-        "shr,str->sht", shaped[:, :, latent_width:], rope_keys, preferred_element_type=jnp.float32
-    )
-    scores = scores * score_scale
-    positions = jnp.arange(latent.shape[1], dtype=jnp.int32)
-    scores = jnp.where(positions[None, None, :] < lengths[:, None, None], scores, -jnp.inf)
-    scores = scores - jnp.max(scores, axis=2, keepdims=True)
-    expsum = jnp.exp(scores)
-    weights_soft = (expsum / jnp.sum(expsum, axis=2, keepdims=True)).astype(jnp.bfloat16)
-    latent_out = jnp.einsum(
-        "sht,stl->shl", weights_soft, latent, preferred_element_type=jnp.float32
-    ).astype(jnp.bfloat16)
-    values = jnp.einsum(
-        "shl,hlv->shv", latent_out, w_absorb, preferred_element_type=jnp.float32
-    ).astype(jnp.bfloat16)
-    return values.reshape(slot_count, -1)
 
 
 MESH = pl.DeviceIdType.MESH
@@ -125,10 +57,15 @@
             copy.wait_send()
 
 
-def experts_kernel(
-    values,
+def decode_kernel(
+    queries,
+    plan,
+    lengths,
     routes,
     gain,
+    cache_latent,
+    cache_rope,
+    w_absorb,
     w_out,
     router,
     w_gate,
@@ -136,6 +73,19 @@
     w_down,
     attended,
     mixed,
+    keys,
+    rope_keys,
+    wa,
+    query_latent,
+    query_rope,
+    query_out,
+    query_in,
+    marks_out,
+    marks,
+    latent_out,
+    values,
+    values_out,
+    values_in,
     wo,
     wr,
     wg,
@@ -168,7 +118,9 @@
     sibling = device(me, other)
     copies = Copies(send_sem, recv_sem)
     width = wg.shape[1]
-    slots = values.shape[0]
+    slots, heads = queries.shape[0], wa.shape[0]
+    latent_width, rope_width = keys.shape[1], rope_keys.shape[1]
+    cap = keys.shape[0] // slots
     half = slots // 2
     tiles = width // 128
     wide = (tiles * 5 + 6) // 7 * 128
@@ -193,6 +145,22 @@
         return pl.ds(pl.multiple_of(slab * width, 128), width)
 
     loads = []
+    group = 16
+    group_keys = group * cap
+    groups = slots // group
+    cache_loads = []
+    for g in range(groups):
+        rows = pl.ds(g * group_keys, group_keys)
+        cache_loads.append(
+            (
+                pltpu.make_async_copy(cache_latent.at[rows], keys.at[rows], load_sem.at[20 + 2 * g]),
+                pltpu.make_async_copy(cache_rope.at[rows], rope_keys.at[rows], load_sem.at[21 + 2 * g]),
+            )
+        )
+        for load in cache_loads[-1]:
+            load.start()
+    absorb_load = pltpu.make_async_copy(w_absorb, wa, load_sem.at[28])
+    absorb_load.start()
     for k, slab in enumerate(slabs):
         loads.append(
             pltpu.make_async_copy(w_out.at[:, columns(slab)], wo.at[:, columns(slab)], load_sem.at[k])
@@ -202,14 +170,150 @@
     for load in loads:
         load.start()
 
+    f32, bf16 = jnp.float32, jnp.bfloat16
+    my_rank = lax.axis_index("dp")
+
+    def iota(shape, axis):
+        return lax.broadcasted_iota(jnp.int32, shape, axis)
+
+    def mark(condition):
+        return jnp.where(condition, 1.0, 0.0)
+
+    def dot(a, b):
+        return jnp.dot(a, b, preferred_element_type=f32)
+
+    shift = slots.bit_length() - 1
+    rank_of, slot_of = plan[...] >> shift, plan[...] & (slots - 1)
+    rank_row = iota((8, slots), 0)
+    earlier = mark(iota((slots, slots), 0) < iota((slots, slots), 1)).astype(bf16)
+    own_rank = jnp.sum(jnp.where(rank_row == my_rank, rank_of, 0).astype(f32), axis=0, keepdims=True)
+    leaving = mark((own_rank == rank_row.astype(f32)) & (rank_row != my_rank))
+    letter = jnp.sum(leaving * dot(leaving.astype(bf16), earlier), axis=0, keepdims=True)
+    away = jnp.sum(leaving, axis=0, keepdims=True)
+    key_row = jnp.where(away > 0.5, own_rank * 2.0 + letter, -1.0)
+    diagonal = iota((slots, slots), 0) == iota((slots, slots), 1)
+    key = jnp.sum(jnp.where(diagonal, key_row, 0.0), axis=1, keepdims=True).astype(jnp.int32)
+    stays = key < 0
+    length = jnp.sum(jnp.where(diagonal, lengths[...].astype(f32), 0.0), axis=1, keepdims=True).astype(jnp.int32)
+
+    arriving = mark((rank_of == my_rank) & (rank_row != my_rank))
+    nth = dot(arriving.astype(bf16), earlier)
+    guest_slot = []
+    for k in range(2):
+        is_kth = (arriving > 0.5) & (jnp.abs(nth - k) < 0.5)
+        guest_slot.append(jnp.sum(jnp.where(is_kth, slot_of + 1, 0).astype(f32), axis=1, keepdims=True) - 1.0)
+
+    def letter_places(axis, shape):
+        place = iota(shape, axis)
+        inner = place & 15
+        return place >> 4, inner >> 1, inner & 1, inner < 2 * heads
+
+    for h in range(heads):
+        start = h * (latent_width + rope_width)
+        query_latent[h] = queries[:, start : start + latent_width]
+        query_rope[h] = queries[:, start + latent_width : start + latent_width + rope_width]
+
+    to_rank, to_head, to_letter, used = letter_places(0, (128, slots))
+    wanted = jnp.where(used, to_rank * 2 + to_letter, -2).astype(f32)
+    chosen = mark(key_row == wanted)
+    out_latent = jnp.zeros((128, latent_width), f32)
+    out_rope = jnp.zeros((128, rope_width), f32)
+    for h in range(heads):
+        rows = jnp.where(to_head == h, chosen, 0.0).astype(bf16)
+        out_latent = out_latent + dot(rows, query_latent[h])
+        out_rope = out_rope + dot(rows, query_rope[h])
+    query_out[:, :, 0:latent_width] = out_latent.astype(bf16).reshape(8, 16, latent_width)
+    query_out[:, :, latent_width:] = (
+        jnp.concatenate([out_rope, jnp.zeros((128, 128 - rope_width), f32)], axis=1)
+        .astype(bf16)
+        .reshape(8, 16, 128)
+    )
+    experts = iota((slots, marks.shape[2]), 1)
+    named = jnp.zeros(experts.shape, f32)
+    for k in range(routes.shape[1]):
+        named = named + mark(routes[:, k : k + 1] == experts)
+    marks_out[...] = named.astype(bf16)
+    marks[my_rank] = named.astype(bf16)
+    query_in[my_rank] = jnp.zeros(query_in.shape[1:], bf16)
+    values_in[my_rank] = jnp.zeros(values_in.shape[1:], bf16)
+
     peers = [sibling]
     for axis in AXES:
         peers += [device(moved(me, axis, k), core) for k in (1, 2, 3)]
     peers += [device(slab_chip(dx, 1), core) for dx in (1, 2, 3)]
+    rank_offsets = [(dz, dy) for dz in range(2) for dy in range(4) if (dz, dy) != (0, 0)]
+
+    def rank_chip(dz, dy):
+        z = me["z"] // 2 * 2 + (me["z"] + dz) % 2
+        return {**me, "z": z, "y": (me["y"] + dy) % 4}
+
+    peers += [device(rank_chip(1, dy), core) for dy in (1, 2, 3)]
     barrier = pltpu.get_barrier_semaphore()
     for peer in peers:
         pl.semaphore_signal(barrier, inc=1, device_id=peer, device_id_type=MESH)
     pl.semaphore_wait(barrier, len(peers))
+
+    from_ranks = []
+    for dz, dy in rank_offsets:
+        chip = rank_chip(dz, dy)
+        to = device(chip, core)
+        from_ranks.append(copies.start(query_out.at[to[0]], query_in.at[my_rank], to))
+    from_marks = []
+    for dz, dy in rank_offsets:
+        from_marks.append(copies.start(marks_out, marks.at[my_rank], device(rank_chip(dz, dy), core)))
+
+    from_rank, from_head, from_letter, used = letter_places(1, (8, 128))
+    guests = jnp.where(from_letter == 0, guest_slot[0], guest_slot[1])
+    guests = jnp.where((from_rank == iota((8, 128), 0)) & used, guests + 1.0, 0.0)
+    guests = jnp.sum(guests, axis=0, keepdims=True) - 1.0
+    _, from_head, _, _ = letter_places(1, (slots, 128))
+    is_guest = mark(guests == iota((slots, 128), 0).astype(f32))
+    for copy in from_ranks:
+        copy.wait_recv()
+    came = query_in[...].reshape(128, query_in.shape[2])
+    for h in range(heads):
+        rows = jnp.where(from_head == h, is_guest, 0.0).astype(bf16)
+        guest = dot(rows, came)
+        query_latent[h] = jnp.where(stays, query_latent[h].astype(f32), guest[:, :latent_width]).astype(bf16)
+        query_rope[h] = jnp.where(
+            stays, query_rope[h].astype(f32), guest[:, latent_width : latent_width + rope_width]
+        ).astype(bf16)
+
+    score_scale = (VDIM + rope_width) ** -0.5
+    rows_shape = (heads * group, group_keys)
+    position = iota(rows_shape, 1) - iota(rows_shape, 0) % group * cap
+    contract_last = (((1,), (1,)), ((), ()))
+    for g in range(groups):
+        for load in cache_loads[g]:
+            load.wait()
+        mine = pl.ds(g * group, group)
+        q_latent = query_latent[:, mine, :].reshape(heads * group, latent_width)
+        q_rope = query_rope[:, mine, :].reshape(heads * group, rope_width)
+        here = pl.ds(g * group_keys, group_keys)
+        scores = lax.dot_general(q_latent, keys[here, :], contract_last, preferred_element_type=f32)
+        scores = scores + lax.dot_general(q_rope, rope_keys[here, :], contract_last, preferred_element_type=f32)
+        limit = jnp.concatenate([length[g * group : (g + 1) * group]] * heads, axis=0)
+        seen = (position >= 0) & (position < limit)
+        scores = jnp.where(seen, scores * score_scale, -jnp.inf)
+        raised = jnp.exp(scores - jnp.max(scores, axis=1, keepdims=True))
+        probs = (raised / jnp.sum(raised, axis=1, keepdims=True)).astype(bf16)
+        latent_out[:, mine, :] = dot(probs, keys[here, :]).astype(bf16).reshape(heads, group, latent_width)
+    absorb_load.wait()
+    for h in range(heads):
+        values[:, h * VDIM : (h + 1) * VDIM] = dot(latent_out[h], wa[h]).astype(bf16)
+
+    guest_column = jnp.concatenate(guest_slot, axis=0)
+    select = mark(guest_column == iota((16, slots), 1).astype(f32)).astype(bf16)
+    values_out[...] = dot(select, values[...]).astype(bf16)
+    from_ranks = []
+    for dz, dy in rank_offsets:
+        from_ranks.append(copies.start(values_out, values_in.at[my_rank], device(rank_chip(dz, dy), core)))
+    for copy in from_ranks:
+        copy.wait_recv()
+    place = (key >> 1) * 16 + (key & 1) * 8 + my_rank
+    back = mark((iota((slots, 128), 1) == place) & (key >= 0)).astype(bf16)
+    returned = dot(back, values_in[...].reshape(128, values_in.shape[2]))
+    values[...] = jnp.where(stays, values[...].astype(f32), returned).astype(bf16)
 
     from_sibling = []
     for k, slab in enumerate(slabs):
@@ -314,10 +418,9 @@
     scores = score_sum[...] * scale
     affinity = 1.0 / (1.0 + jnp.exp(-scores))
     experts = lax.broadcasted_iota(jnp.int32, scores.shape, 1)
-    named = jnp.zeros(scores.shape, jnp.float32)
-    for k in range(routes.shape[1]):
-        named = named + jnp.where(routes[:, k : k + 1] == experts, 1.0, 0.0)
-    chosen = affinity * named
+    for copy in from_marks:
+        copy.wait_recv()
+    chosen = affinity * marks[...].reshape(scores.shape).astype(f32)
     mine = jnp.sum(jnp.where(experts == lax.axis_index("ep"), chosen, 0.0), axis=1, keepdims=True)
     weight = route_scale * mine / jnp.sum(chosen, axis=1, keepdims=True)
     gate = gate_sum[...] * scale
@@ -454,8 +557,14 @@
     copies.finish()
 
 
-def run_experts(values, routes, gain, w_out, router, w_gate, w_up, w_down):
-    slots, heads_width = values.shape
+def run_decode(
+    queries, plan, lengths, routes, gain, cache_latent, cache_rope, w_absorb, w_out, router, w_gate, w_up, w_down
+):
+    slots = queries.shape[0]
+    cap, latent_width = cache_latent.shape[1:]
+    rope_width = cache_rope.shape[2]
+    heads = w_absorb.shape[0]
+    heads_width = w_out.shape[0]
     model = w_out.shape[1]
     width = model // 8
     half = slots // 2
@@ -468,14 +577,27 @@
     vmem = pl.BlockSpec(memory_space=pltpu.VMEM)
     hbm = pl.BlockSpec(memory_space=pl.ANY)
     return pl.pallas_call(
-        experts_kernel,
+        decode_kernel,
         out_shape=(
             jax.ShapeDtypeStruct((slots, model), bf16),
             jax.ShapeDtypeStruct((2, 16, unit_cols), bf16),
         ),
-        in_specs=[vmem, vmem, vmem, hbm, hbm, hbm, hbm, hbm],
+        in_specs=[vmem] * 5 + [hbm] * 8,
         out_specs=(hbm, vmem),
         scratch_shapes=[
+            pltpu.VMEM((slots * cap, latent_width), bf16),
+            pltpu.VMEM((slots * cap, rope_width), bf16),
+            pltpu.VMEM(w_absorb.shape, bf16),
+            pltpu.VMEM((heads, slots, latent_width), bf16),
+            pltpu.VMEM((heads, slots, rope_width), bf16),
+            pltpu.VMEM((8, 16, latent_width + 128), bf16),
+            pltpu.VMEM((8, 16, latent_width + 128), bf16),
+            pltpu.VMEM((slots, experts), bf16),
+            pltpu.VMEM((8, slots, experts), bf16),
+            pltpu.VMEM((heads, slots, latent_width), bf16),
+            pltpu.VMEM((slots, heads_width), bf16),
+            pltpu.VMEM((16, heads_width), bf16),
+            pltpu.VMEM((8, 16, heads_width), bf16),
             pltpu.VMEM((heads_width, model), bf16),
             pltpu.VMEM((8, width, experts), bf16),
             pltpu.VMEM((8, width, hidden), bf16),
@@ -499,18 +621,23 @@
             pltpu.VMEM((3, 4, 16, share), bf16),
             pltpu.VMEM((3, 3, 16, share), bf16),
             pltpu.VMEM((2, 16, unit_cols), bf16),
-            pltpu.SemaphoreType.DMA((20,)),
-            pltpu.SemaphoreType.DMA((112,)),
-            pltpu.SemaphoreType.DMA((112,)),
+            pltpu.SemaphoreType.DMA((32,)),
+            pltpu.SemaphoreType.DMA((128,)),
+            pltpu.SemaphoreType.DMA((128,)),
         ],
         compiler_params=pltpu.CompilerParams(
             collective_id=0, has_side_effects=True, vmem_limit_bytes=60 * 1024 * 1024
         ),
-        name="experts",
+        name="decode",
     )(
-        values,
+        queries,
+        plan,
+        lengths,
         routes,
         gain.reshape(8, 1, width),
+        cache_latent.reshape(slots * cap, latent_width),
+        cache_rope.reshape(slots * cap, rope_width),
+        w_absorb,
         w_out,
         router.reshape(8, width, experts),
         w_gate.reshape(8, width, hidden),
@@ -534,11 +661,21 @@
     w_up,
     w_down,
 ):
-    all_routes = lax.all_gather(routes, "dp", axis=0, tiled=True)
-    latent, rope_keys, lengths = move_caches(cache_latent, cache_rope, cache_len, move_plan)
-    values = attend(queries, latent, rope_keys, lengths, w_absorb)
-    attended, mixed = run_experts(
-        values, all_routes, norm_gain, w_out, router, w_gate[0], w_up[0], w_down[0]
+    slots = cache_len.shape[0]
+    attended, mixed = run_decode(
+        queries,
+        move_plan.reshape(-1, slots),
+        cache_len.reshape(1, slots),
+        routes,
+        norm_gain,
+        cache_latent,
+        cache_rope,
+        w_absorb,
+        w_out,
+        router,
+        w_gate[0],
+        w_up[0],
+        w_down[0],
     )
     core = lax.axis_index("ep") % 2
     quarters = mixed.reshape(2, 2, 2, 4, mixed.shape[-1])

time: 182 us -> 113 us (0.62)
  blocking collectives: 22.2 us -> 0 us
  local copies, waits for them, and re-layouts: 26.1 us -> 11.4 us
  starting transfers between devices: 14.1 us -> 0 us
  waiting for transfers between devices: 9.5 us -> 0 us
  Pallas kernels: 92.4 us -> 101 us
  other arithmetic: 8.19 us -> 0 us
  matrix products: 8.1 us -> 0 us
    all_gather x1 -> x0, blocking collectives: 22.2 us -> none  [per_device(): all_routes = lax.all_gather(routes, 'dp', axis=0, tiled=True)]
    gather x6 -> x0, local copies, waits for them, and re-layouts: 17 us -> none  [the longest x1 6.12 us: move_caches(): latent_pool[pool_index]]
    all_to_all x3 -> x0, starting transfers between devices: 14.1 us -> none  [the longest x1 6.37 us: move_caches(): lax.all_to_all(packed[2], 'dp', split_axis=0, concat_axis=0, tiled=True)]
    all_to_all x3 -> x0, waiting for transfers between devices: 9.5 us -> none  [the longest x1 7.07 us: move_caches(): lax.all_to_all(packed[0], 'dp', split_axis=0, concat_axis=0, tiled=True)]
    pallas_call x1, Pallas kernels: 92.4 us -> 101 us  [run_decode(): pl.pallas_call(decode_kernel, out_shape=(jax.ShapeDtypeStruct((slots, mod...]
    dot_general x4 -> x0, matrix products: 8.1 us -> none  [the longest x1 3.93 us: attend(): jnp.einsum('shl,stl->sht', shaped[:, :, :latent_width], latent, preferred...]
    concatenate x3 -> x0, other arithmetic: 7.19 us -> none  [the longest x1 5.78 us: move_caches(): jnp.concatenate([cache_latent, got_latent.reshape((-1,) + cache_latent.sh...]
    unnamed x14 -> x4, local copies, waits for them, and re-layouts: 3.89 us -> 8.46 us
  transfers between devices with their start and end apart: 3 -> 0, of which waited for: 2 -> 0; matrix products, arithmetic and copies ran while one was open for 8% -> 0% of each run, Pallas kernels for 0% -> 0%
where the time goes in v2:
time: 113 us
  Pallas kernels  101 us (89%)
  local copies, waits for them, and re-layouts  11.4 us (10%)
    pallas_call x1, Pallas kernels, run_decode(): pl.pallas_call(decode_kernel, out_shape=(jax.ShapeDtypeStruct((slots, mod...  101 us
    unnamed x4, local copies, waits for them, and re-layouts  8.46 us

profile of v2, /device:TPU:1, one launch (start us, length us, event | category | flops | bytes accessed | tf_op | source)
XLA Modules:
  0.0 112.9 jit_solution(1857385061451699206)
XLA Ops:
  0.6 1.3 %reshape.28.plan = s32[8,64]{1,0:T(8,128)} reshape(s32[512]{0:T(512)} %param.17) | data formatting | bytes 4096 | tf_op jit(solution)/shard_map/reshape | solution.py:667
  2.0 1.4 %copy.20.routes = s32[64,8]{1,0:T(8,128)} copy(s32[64,8]{0,1:T(8,128)} %param.22) | data formatting | bytes 4096 | tf_op args[9]
  3.4 2.4 %copy.18 = bf16[64,80,64]{2,1,0:T(8,128)(2,1)} copy(bf16[64,80,64]{1,2,0:T(8,128)(2,1)} %param.15) | data formatting | bytes 1310720 | tf_op args[2]
  5.8 2.5 %copy.19 = bf16[7168,16]{1,0:T(8,128)(2,1)} copy(bf16[7168,16]{0,1:T(8,128)(2,1)} %param.21) | data formatting | bytes 458752 | tf_op args[8]
  8.3 100.8 %decode.1 = (bf16[64,7168]{1,0:T(8,128)(2,1)}, bf16[2,16,1792]{2,1,0:T(8,128)(2,1)}) custom-call(bf16[64,2304]{1,0:T(8,128)(2,1)} %queries.1, s32[8,64]{1,0:T(8,128)} %reshape.28.plan, s32[1,64]{1,0:T(1,128)} %bitcast.23, s32[64,8]{1,0:T(8,128)} %copy.20.routes, f32[8,1,896]{2,1,0:T(1,128)} %bitcast.22, bf16[5120,512]{1,0:T(8,128)(2,1)} %bitcast.17, ...), custom_call_target="tpu_custom_call" | custom-call | tf_op jit(solution)/shard_map/decode/pallas_call | solution.py:579
  109.1 0.9 reshape.34
  110.1 0.7 constant_dynamic-slice_fusion
  110.7 2.2 %copy.24 = bf16[64,7168]{1,0:T(8,128)(2,1)} copy(bf16[64,7168]{1,0:T(8,128)(2,1)} %get-tuple-element.8) | data formatting | bytes 1835008

commit v3 on v2

--- a/solution.py
+++ b/solution.py
@@ -154,7 +154,9 @@
         cache_loads.append(
             (
                 pltpu.make_async_copy(cache_latent.at[rows], keys.at[rows], load_sem.at[20 + 2 * g]),
-                pltpu.make_async_copy(cache_rope.at[rows], rope_keys.at[rows], load_sem.at[21 + 2 * g]),
+                pltpu.make_async_copy(
+                    cache_rope.at[pl.ds(g * group, group)], rope_keys.at[pl.ds(g * group, group)], load_sem.at[21 + 2 * g]
+                ),
             )
         )
         for load in cache_loads[-1]:
@@ -183,7 +185,8 @@
         return jnp.dot(a, b, preferred_element_type=f32)
 
     shift = slots.bit_length() - 1
-    rank_of, slot_of = plan[...] >> shift, plan[...] & (slots - 1)
+    sources = jnp.concatenate([plan[:, r * slots : (r + 1) * slots] for r in range(8)], axis=0)
+    rank_of, slot_of = sources >> shift, sources & (slots - 1)
     rank_row = iota((8, slots), 0)
     earlier = mark(iota((slots, slots), 0) < iota((slots, slots), 1)).astype(bf16)
     own_rank = jnp.sum(jnp.where(rank_row == my_rank, rank_of, 0).astype(f32), axis=0, keepdims=True)
@@ -230,8 +233,9 @@
     )
     experts = iota((slots, marks.shape[2]), 1)
     named = jnp.zeros(experts.shape, f32)
-    for k in range(routes.shape[1]):
-        named = named + mark(routes[:, k : k + 1] == experts)
+    for k in range(routes.shape[0]):
+        route = jnp.sum(jnp.where(diagonal, routes[k : k + 1, :], 0).astype(f32), axis=1, keepdims=True)
+        named = named + mark(route.astype(jnp.int32) == experts)
     marks_out[...] = named.astype(bf16)
     marks[my_rank] = named.astype(bf16)
     query_in[my_rank] = jnp.zeros(query_in.shape[1:], bf16)
@@ -291,7 +295,8 @@
         q_rope = query_rope[:, mine, :].reshape(heads * group, rope_width)
         here = pl.ds(g * group_keys, group_keys)
         scores = lax.dot_general(q_latent, keys[here, :], contract_last, preferred_element_type=f32)
-        scores = scores + lax.dot_general(q_rope, rope_keys[here, :], contract_last, preferred_element_type=f32)
+        rotary = jnp.concatenate([rope_keys[g * group + k] for k in range(group)], axis=1)
+        scores = scores + dot(q_rope, rotary)
         limit = jnp.concatenate([length[g * group : (g + 1) * group]] * heads, axis=0)
         seen = (position >= 0) & (position < limit)
         scores = jnp.where(seen, scores * score_scale, -jnp.inf)
@@ -412,7 +417,12 @@
         gained = (rows * gain[slab]).astype(jnp.bfloat16)
         gate_sum[...] += jnp.dot(gained, wg[slab], preferred_element_type=jnp.float32)
         up_sum[...] += jnp.dot(gained, wu[slab], preferred_element_type=jnp.float32)
-        score_sum[...] += jnp.dot(gained, wr[slab], preferred_element_type=jnp.float32)
+        score_sum[...] += lax.dot_general(
+            gained,
+            wr[:, pl.ds(pl.multiple_of(slab * width, 128), width)],
+            contract_last,
+            preferred_element_type=f32,
+        )
 
     scale = lax.rsqrt(square_sum[...] * (1.0 / (8 * width)) + epsilon)
     scores = score_sum[...] * scale
@@ -549,9 +559,14 @@
             total = total + parts_three[p, k, :, pl.ds(0, width_p)].astype(jnp.float32)
         final_half[0, :, pl.ds(*out_cols[p])] = total.astype(jnp.bfloat16)
     last_copy = copies.start(final_half.at[0], final_half.at[1], sibling)
-    mixed[core] = final_half[0]
     last_copy.wait_recv()
-    mixed[other] = final_half[1]
+    for side, column_half in enumerate((core, other)):
+        both = final_half[side].astype(f32)
+        for quarter in range(2):
+            eight = both[quarter * 8 : quarter * 8 + 8]
+            own = jnp.where(core == 0, eight[0:4], eight[4:8])
+            start = pl.multiple_of(column_half * (2 * unit_cols) + quarter * unit_cols, 128)
+            mixed[:, pl.ds(start, unit_cols)] = own.astype(bf16)
     for copy in rank_copies:
         copy.wait()
     copies.finish()
@@ -580,13 +595,13 @@
         decode_kernel,
         out_shape=(
             jax.ShapeDtypeStruct((slots, model), bf16),
-            jax.ShapeDtypeStruct((2, 16, unit_cols), bf16),
+            jax.ShapeDtypeStruct((4, model), bf16),
         ),
         in_specs=[vmem] * 5 + [hbm] * 8,
         out_specs=(hbm, vmem),
         scratch_shapes=[
             pltpu.VMEM((slots * cap, latent_width), bf16),
-            pltpu.VMEM((slots * cap, rope_width), bf16),
+            pltpu.VMEM((slots, rope_width, cap), bf16),
             pltpu.VMEM(w_absorb.shape, bf16),
             pltpu.VMEM((heads, slots, latent_width), bf16),
             pltpu.VMEM((heads, slots, rope_width), bf16),
@@ -599,7 +614,7 @@
             pltpu.VMEM((16, heads_width), bf16),
             pltpu.VMEM((8, 16, heads_width), bf16),
             pltpu.VMEM((heads_width, model), bf16),
-            pltpu.VMEM((8, width, experts), bf16),
+            pltpu.VMEM((experts, model), bf16),
             pltpu.VMEM((8, width, hidden), bf16),
             pltpu.VMEM((8, width, hidden), bf16),
             pltpu.VMEM((hidden, model), bf16),
@@ -633,17 +648,60 @@
         queries,
         plan,
         lengths,
-        routes,
+        routes.T,
         gain.reshape(8, 1, width),
         cache_latent.reshape(slots * cap, latent_width),
-        cache_rope.reshape(slots * cap, rope_width),
+        cache_rope.transpose(0, 2, 1),
         w_absorb,
         w_out,
-        router.reshape(8, width, experts),
+        router.T,
         w_gate.reshape(8, width, hidden),
         w_up.reshape(8, width, hidden),
         w_down,
     )
+
+
+def copy_kernel(source, small_source, target, small_target, held, small_held, sems):
+    parts = held.shape[0]
+    width = source.shape[1] // parts
+    small_in = pltpu.make_async_copy(small_source, small_held, sems.at[2 * parts])
+    small_in.start()
+    copies_in, copies_out = [], []
+    for k in range(parts):
+        columns = pl.ds(k * width, width)
+        copies_in.append(pltpu.make_async_copy(source.at[:, columns], held.at[k], sems.at[k]))
+        copies_out.append(pltpu.make_async_copy(held.at[k], target.at[:, columns], sems.at[parts + k]))
+        copies_in[-1].start()
+    small_in.wait()
+    small_out = pltpu.make_async_copy(small_held, small_target, sems.at[2 * parts + 1])
+    small_out.start()
+    for copy_in, copy_out in zip(copies_in, copies_out):
+        copy_in.wait()
+        copy_out.start()
+    for copy in copies_out:
+        copy.wait()
+    small_out.wait()
+
+
+def write_out(attended, mixed):
+    hbm = pl.BlockSpec(memory_space=pl.ANY)
+    parts = 4
+    return pl.pallas_call(
+        copy_kernel,
+        out_shape=(
+            jax.ShapeDtypeStruct(attended.shape, attended.dtype),
+            jax.ShapeDtypeStruct(mixed.shape, mixed.dtype),
+        ),
+        in_specs=[hbm, hbm],
+        out_specs=(hbm, hbm),
+        scratch_shapes=[
+            pltpu.VMEM((parts, attended.shape[0], attended.shape[1] // parts), attended.dtype),
+            pltpu.VMEM(mixed.shape, mixed.dtype),
+            pltpu.SemaphoreType.DMA((2 * parts + 2,)),
+        ],
+        compiler_params=pltpu.CompilerParams(vmem_limit_bytes=60 * 1024 * 1024),
+        name="write_out",
+    )(attended, mixed)
 
 
 def per_device(
@@ -664,7 +722,7 @@
     slots = cache_len.shape[0]
     attended, mixed = run_decode(
         queries,
-        move_plan.reshape(-1, slots),
+        move_plan.reshape(1, -1),
         cache_len.reshape(1, slots),
         routes,
         norm_gain,
@@ -677,11 +735,7 @@
         w_up[0],
         w_down[0],
     )
-    core = lax.axis_index("ep") % 2
-    quarters = mixed.reshape(2, 2, 2, 4, mixed.shape[-1])
-    own = lax.dynamic_index_in_dim(quarters, core, 2, keepdims=False)
-    mixture = own.transpose(2, 0, 1, 3).reshape(4, -1)
-    return (attended, mixture)
+    return write_out(attended, mixed)
 
 
 def solution(mesh):

time: 113 us -> 104 us (0.920)
  local copies, waits for them, and re-layouts: 11.4 us -> 0 us
  Pallas kernels: 101 us -> 103 us
    unnamed x4 -> x0, local copies, waits for them, and re-layouts: 8.46 us -> none
    reshape x2 -> x0, local copies, waits for them, and re-layouts: 2.28 us -> none  [the longest x1 1.35 us: per_device(): move_plan.reshape(-1, slots)]
    pallas_call x0 -> x1, Pallas kernels: none -> 2.08 us  [write_out(): pl.pallas_call(copy_kernel, out_shape=(jax.ShapeDtypeStruct(attended.shap...]
where the time goes in v3:
time: 104 us
  Pallas kernels  103 us (99%)
    pallas_call x1, Pallas kernels, run_decode(): pl.pallas_call(decode_kernel, out_shape=(jax.ShapeDtypeStruct((slots, mod...  101 us
    pallas_call x1, Pallas kernels, write_out(): pl.pallas_call(copy_kernel, out_shape=(jax.ShapeDtypeStruct(attended.shap...  2.08 us

profile of v3, /device:TPU:1, one launch (start us, length us, event | category | flops | bytes accessed | tf_op | source)
XLA Modules:
  0.0 103.6 jit_solution(5684284347776605568)
XLA Ops:
  0.6 100.8 %decode.1 = (bf16[64,7168]{1,0:T(8,128)(2,1)}, bf16[4,7168]{1,0:T(4,128)(2,1)}) custom-call(bf16[64,2304]{1,0:T(8,128)(2,1)} %queries.1, s32[1,512]{1,0:T(1,128)} %bitcast.18, s32[1,64]{1,0:T(1,128)} %bitcast.19, s32[8,64]{1,0:T(8,128)} %bitcast.17, f32[8,1,896]{2,1,0:T(1,128)} %bitcast.16, bf16[5120,512]{1,0:T(8,128)(2,1)} %bitcast.10, ...), custom_call_target="tpu_custom_call" | custom-call | tf_op jit(solution)/shard_map/decode/pallas_call | solution.py:594
  101.5 2.1 %write_out.1 = (bf16[64,7168]{1,0:T(8,128)(2,1)}, bf16[4,7168]{1,0:T(4,128)(2,1)}) custom-call(bf16[64,7168]{1,0:T(8,128)(2,1)} %get-tuple-element.4.source, bf16[4,7168]{1,0:T(4,128)(2,1)} %get-tuple-element.5.small_source), custom_call_target="tpu_custom_call" | custom-call | tf_op jit(solution)/shard_map/write_out/pallas_call | solution.py:689

commit v4 on v3

--- a/solution.py
+++ b/solution.py
@@ -58,11 +58,11 @@
 
 
 def decode_kernel(
-    queries,
     plan,
     lengths,
     routes,
-    gain,
+    queries_in,
+    gain_in,
     cache_latent,
     cache_rope,
     w_absorb,
@@ -73,8 +73,11 @@
     w_down,
     attended,
     mixed,
+    queries,
+    gain,
     keys,
     rope_keys,
+    rotary,
     wa,
     query_latent,
     query_rope,
@@ -95,10 +98,6 @@
     core_terms,
     slab_terms,
     tokens,
-    gate_sum,
-    up_sum,
-    score_sum,
-    square_sum,
     act,
     partial,
     core_partial,
@@ -117,7 +116,7 @@
     other = 1 - core
     sibling = device(me, other)
     copies = Copies(send_sem, recv_sem)
-    width = wg.shape[1]
+    width = wg.shape[1] // 2
     slots, heads = queries.shape[0], wa.shape[0]
     latent_width, rope_width = keys.shape[1], rope_keys.shape[1]
     cap = keys.shape[0] // slots
@@ -144,6 +143,24 @@
     def columns(slab):
         return pl.ds(pl.multiple_of(slab * width, 128), width)
 
+    peers = [sibling]
+    for axis in AXES:
+        peers += [device(moved(me, axis, k), core) for k in (1, 2, 3)]
+    peers += [device(slab_chip(dx, 1), core) for dx in (1, 2, 3)]
+    rank_offsets = [(dz, dy) for dz in range(2) for dy in range(4) if (dz, dy) != (0, 0)]
+
+    def rank_chip(dz, dy):
+        z = me["z"] // 2 * 2 + (me["z"] + dz) % 2
+        return {**me, "z": z, "y": (me["y"] + dy) % 4}
+
+    peers += [device(rank_chip(1, dy), core) for dy in (1, 2, 3)]
+    barrier = pltpu.get_barrier_semaphore()
+    for peer in peers:
+        pl.semaphore_signal(barrier, inc=1, device_id=peer, device_id_type=MESH)
+
+    query_load = pltpu.make_async_copy(queries_in, queries, load_sem.at[50])
+    query_load.start()
+    gain_load = pltpu.make_async_copy(gain_in, gain, load_sem.at[51])
     loads = []
     group = 16
     group_keys = group * cap
@@ -169,6 +186,7 @@
         )
     for k, (source, target) in enumerate(((w_gate, wg), (w_up, wu), (router, wr), (w_down, wd))):
         loads.append(pltpu.make_async_copy(source, target, load_sem.at[8 + k]))
+    loads.append(gain_load)
     for load in loads:
         load.start()
 
@@ -211,6 +229,7 @@
         inner = place & 15
         return place >> 4, inner >> 1, inner & 1, inner < 2 * heads
 
+    query_load.wait()
     for h in range(heads):
         start = h * (latent_width + rope_width)
         query_latent[h] = queries[:, start : start + latent_width]
@@ -231,32 +250,17 @@
         .astype(bf16)
         .reshape(8, 16, 128)
     )
-    experts = iota((slots, marks.shape[2]), 1)
+    experts = iota((slots, marks.shape[3]), 1)
     named = jnp.zeros(experts.shape, f32)
     for k in range(routes.shape[0]):
         route = jnp.sum(jnp.where(diagonal, routes[k : k + 1, :], 0).astype(f32), axis=1, keepdims=True)
         named = named + mark(route.astype(jnp.int32) == experts)
-    marks_out[...] = named.astype(bf16)
-    marks[my_rank] = named.astype(bf16)
+    marks_out[...] = named.astype(bf16).reshape(marks_out.shape)
+    marks[my_rank] = marks_out[...]
     query_in[my_rank] = jnp.zeros(query_in.shape[1:], bf16)
     values_in[my_rank] = jnp.zeros(values_in.shape[1:], bf16)
 
-    peers = [sibling]
-    for axis in AXES:
-        peers += [device(moved(me, axis, k), core) for k in (1, 2, 3)]
-    peers += [device(slab_chip(dx, 1), core) for dx in (1, 2, 3)]
-    rank_offsets = [(dz, dy) for dz in range(2) for dy in range(4) if (dz, dy) != (0, 0)]
-
-    def rank_chip(dz, dy):
-        z = me["z"] // 2 * 2 + (me["z"] + dz) % 2
-        return {**me, "z": z, "y": (me["y"] + dy) % 4}
-
-    peers += [device(rank_chip(1, dy), core) for dy in (1, 2, 3)]
-    barrier = pltpu.get_barrier_semaphore()
-    for peer in peers:
-        pl.semaphore_signal(barrier, inc=1, device_id=peer, device_id_type=MESH)
     pl.semaphore_wait(barrier, len(peers))
-
     from_ranks = []
     for dz, dy in rank_offsets:
         chip = rank_chip(dz, dy)
@@ -272,6 +276,11 @@
     guests = jnp.sum(guests, axis=0, keepdims=True) - 1.0
     _, from_head, _, _ = letter_places(1, (slots, 128))
     is_guest = mark(guests == iota((slots, 128), 0).astype(f32))
+    for g in range(groups):
+        for load in cache_loads[g]:
+            load.wait()
+    for g in range(groups):
+        rotary[g] = jnp.concatenate([rope_keys[g * group + k] for k in range(group)], axis=1)
     for copy in from_ranks:
         copy.wait_recv()
     came = query_in[...].reshape(128, query_in.shape[2])
@@ -288,15 +297,12 @@
     position = iota(rows_shape, 1) - iota(rows_shape, 0) % group * cap
     contract_last = (((1,), (1,)), ((), ()))
     for g in range(groups):
-        for load in cache_loads[g]:
-            load.wait()
         mine = pl.ds(g * group, group)
         q_latent = query_latent[:, mine, :].reshape(heads * group, latent_width)
         q_rope = query_rope[:, mine, :].reshape(heads * group, rope_width)
         here = pl.ds(g * group_keys, group_keys)
         scores = lax.dot_general(q_latent, keys[here, :], contract_last, preferred_element_type=f32)
-        rotary = jnp.concatenate([rope_keys[g * group + k] for k in range(group)], axis=1)
-        scores = scores + dot(q_rope, rotary)
+        scores = scores + dot(q_rope, rotary[g])
         limit = jnp.concatenate([length[g * group : (g + 1) * group]] * heads, axis=0)
         seen = (position >= 0) & (position < limit)
         scores = jnp.where(seen, scores * score_scale, -jnp.inf)
@@ -321,8 +327,9 @@
     values[...] = jnp.where(stays, values[...].astype(f32), returned).astype(bf16)
 
     from_sibling = []
+    for load in loads[:8]:
+        load.wait()
     for k, slab in enumerate(slabs):
-        loads[k].wait()
         head_terms = jnp.dot(values[...], wo[:, columns(slab)], preferred_element_type=jnp.float32)
         terms[k] = head_terms.astype(jnp.bfloat16).reshape(2, half, width)
         from_sibling.append(copies.start(terms.at[k, other], core_terms.at[k], sibling))
@@ -338,104 +345,123 @@
     for k, copy in enumerate(from_slabs):
         copy.wait_recv()
         total = total + slab_terms[k].astype(jnp.float32)
-    own_rows = pl.ds(pl.multiple_of(core * half, 16), half)
-    tokens[me["x"], me["z"], me["y"], own_rows, :] = total.astype(jnp.bfloat16)
+    tokens[me["x"], me["z"], me["y"], core] = total.astype(jnp.bfloat16)
 
     def block(p, where):
         first, count = piece_rows[p]
-        rows = pl.ds(pl.multiple_of(core * half + first, 16), count)
-        return pick(tokens, where, (rows, pl.ds(*piece_cols[p])))
+        return pick(tokens, where, (core, pl.ds(first, count), pl.ds(*piece_cols[p])))
 
     def spread(p, where, to):
         return copies.start(block(p, where), block(p, where), to)
 
-    to_core = []
-    phase_one, phase_two = {}, {}
-    for p, (first, second, last) in enumerate(ORDERS):
-        phase_one[p] = [spread(p, me, device(moved(me, first, k), core)) for k in (1, 3, 2)]
-    for p, (first, second, last) in enumerate(ORDERS):
-        for copy in phase_one[p]:
+    pieces = range(3)
+    rights = [device(moved(me, order[2], 1), core) for order in ORDERS]
+    lefts = [device(moved(me, order[2], 3), core) for order in ORDERS]
+    before = [(me[order[2]] + 3) % 4 for order in ORDERS]
+    after = [(me[order[2]] + 1) % 4 for order in ORDERS]
+    across = [(me[order[2]] + 2) % 4 for order in ORDERS]
+    here = [me[order[2]] for order in ORDERS]
+
+    def group_at(p, k, last):
+        second = ORDERS[p][1]
+        return {second: (me[second] + 4 - k) % 4, ORDERS[p][2]: last}
+
+    one = [
+        [spread(p, me, device(moved(me, ORDERS[p][0], k), core)) for k in (1, 3, 2)] for p in pieces
+    ]
+    two = [{} for p in pieces]
+    to_right, to_left = [{} for p in pieces], [{} for p in pieces]
+    far, to_core = [[] for p in pieces], []
+
+    def near(p, k):
+        where = group_at(p, k, here[p])
+        to_right[p][k] = spread(p, where, rights[p])
+        to_left[p][k] = spread(p, where, lefts[p])
+
+    for p in pieces:
+        for copy in one[p]:
             copy.wait_recv()
-        where = {second: me[second], last: me[last]}
-        phase_two[p] = [spread(p, where, device(moved(me, second, k), core)) for k in (1, 3, 2)]
-    near = {}
-    for p, (first, second, last) in enumerate(ORDERS):
-        for copy in phase_two[p]:
-            copy.wait_recv()
-        parts = [{last: me[last], second: pl.ds(0, 2)}, {last: me[last], second: pl.ds(2, 2)}]
-        right, left = device(moved(me, last, 1), core), device(moved(me, last, 3), core)
-        right_a, left_b = spread(p, parts[0], right), spread(p, parts[1], left)
-        right_b, left_a = spread(p, parts[1], right), spread(p, parts[0], left)
-        near[p] = (right_a, right_b, left_a, left_b)
-        to_core.append(spread(p, {last: me[last]}, sibling))
-    far = {}
-    for p, (first, second, last) in enumerate(ORDERS):
-        right_a, right_b, left_a, left_b = near[p]
-        right, left = device(moved(me, last, 1), core), device(moved(me, last, 3), core)
-        before, after = (me[last] + 3) % 4, (me[last] + 1) % 4
-        right_a.wait_recv()
-        forward_a = spread(p, {last: before, second: pl.ds(0, 2)}, right)
-        left_b.wait_recv()
-        forward_b = spread(p, {last: after, second: pl.ds(2, 2)}, left)
-        far[p] = (forward_a, forward_b)
-    for p, (first, second, last) in enumerate(ORDERS):
-        right_a, right_b, left_a, left_b = near[p]
-        before, after = (me[last] + 3) % 4, (me[last] + 1) % 4
-        right_b.wait_recv()
-        to_core.append(spread(p, {last: before}, sibling))
-        left_a.wait_recv()
-        to_core.append(spread(p, {last: after}, sibling))
-    for p, (first, second, last) in enumerate(ORDERS):
+        for k in (1, 3, 2):
+            two[p][k] = spread(p, group_at(p, 0, here[p]), device(moved(me, ORDERS[p][1], k), core))
+        near(p, 0)
+    for k in (1, 3):
+        for p in pieces:
+            two[p][k].wait_recv()
+            near(p, k)
+    for p in pieces:
+        to_right[p][0].wait_recv()
+        far[p].append(spread(p, group_at(p, 0, before[p]), rights[p]))
+    for p in pieces:
+        two[p][2].wait_recv()
+        near(p, 2)
+        to_core.append(spread(p, {ORDERS[p][2]: here[p]}, sibling))
+    for p in pieces:
+        to_left[p][3].wait_recv()
+        far[p].append(spread(p, group_at(p, 3, after[p]), lefts[p]))
+        to_right[p][1].wait_recv()
+        far[p].append(spread(p, group_at(p, 1, before[p]), rights[p]))
+    for p in pieces:
+        to_left[p][2].wait_recv()
+        far[p].append(spread(p, group_at(p, 2, after[p]), lefts[p]))
+    for p in pieces:
+        for k in (3, 2):
+            to_right[p][k].wait_recv()
+        to_core.append(spread(p, {ORDERS[p][2]: before[p]}, sibling))
+        for k in (0, 1):
+            to_left[p][k].wait_recv()
+        to_core.append(spread(p, {ORDERS[p][2]: after[p]}, sibling))
+    for p in pieces:
         for copy in far[p]:
             copy.wait_recv()
-        to_core.append(spread(p, {last: (me[last] + 2) % 4}, sibling))
+        to_core.append(spread(p, {ORDERS[p][2]: across[p]}, sibling))
+
+    for load in loads[8:]:
+        load.wait()
+    for copy in from_marks:
+        copy.wait_recv()
+
+    def products(side):
+        square_sum = jnp.zeros((8 * half, 128), f32)
+        gate, up, score = 0.0, 0.0, 0.0
+        for x in range(4):
+            rows = [tokens[x, pl.ds(zh * 2, 2), :, side].reshape(8 * half, width) for zh in range(2)]
+            rows = jnp.concatenate(rows, axis=1).astype(f32)
+            for k in range(2 * width // 128):
+                part = rows[:, k * 128 : (k + 1) * 128]
+                square_sum = square_sum + part * part
+            gained = (rows * gain[x]).astype(bf16)
+            gate = gate + dot(gained, wg[x])
+            up = up + dot(gained, wu[x])
+            score = score + lax.dot_general(
+                gained, wr[:, x * 2 * width : (x + 1) * 2 * width], contract_last, preferred_element_type=f32
+            )
+
+        scale = lax.rsqrt(jnp.sum(square_sum, axis=1, keepdims=True) * (1.0 / (8 * width)) + epsilon)
+        affinity = 1.0 / (1.0 + jnp.exp(-score * scale))
+        chosen = affinity * marks[:, side].reshape(affinity.shape).astype(f32)
+        expert = iota(affinity.shape, 1)
+        mine = jnp.sum(jnp.where(expert == lax.axis_index("ep"), chosen, 0.0), axis=1, keepdims=True)
+        weight = route_scale * mine / jnp.sum(chosen, axis=1, keepdims=True)
+        gate = gate * scale
+        hidden = gate / (1.0 + jnp.exp(-gate)) * (up * scale) * weight
+        act[:, side] = hidden.astype(bf16).reshape(8, half, hidden.shape[1])
+
+    products(core)
     for copy in to_core:
         copy.wait_recv()
 
     rank_copies = []
     for slab in range(8):
-        rank_copies.append(
-            pltpu.make_async_copy(
-                tokens.at[slab // 2, slab % 2 * 2 + me["z"] % 2, me["y"]],
-                attended.at[:, pl.ds(slab * width, width)],
-                load_sem.at[12 + slab],
+        for side in range(2):
+            rank_copies.append(
+                pltpu.make_async_copy(
+                    tokens.at[slab // 2, slab % 2 * 2 + me["z"] % 2, me["y"], side],
+                    attended.at[pl.ds(side * half, half), pl.ds(slab * width, width)],
+                    load_sem.at[32 + 2 * slab + side],
+                )
             )
-        )
-        rank_copies[-1].start()
-
-    for load in loads[8:]:
-        load.wait()
-    gate_sum[...] = jnp.zeros_like(gate_sum)
-    up_sum[...] = jnp.zeros_like(up_sum)
-    score_sum[...] = jnp.zeros_like(score_sum)
-    square_sum[...] = jnp.zeros_like(square_sum)
-
-    @pl.loop(0, 8)
-    def _(slab):
-        rows = tokens[slab // 2, pl.ds(slab % 2 * 2, 2)].reshape(8 * slots, width).astype(jnp.float32)
-        square_sum[...] += jnp.sum(rows * rows, axis=1, keepdims=True)
-        gained = (rows * gain[slab]).astype(jnp.bfloat16)
-        gate_sum[...] += jnp.dot(gained, wg[slab], preferred_element_type=jnp.float32)
-        up_sum[...] += jnp.dot(gained, wu[slab], preferred_element_type=jnp.float32)
-        score_sum[...] += lax.dot_general(
-            gained,
-            wr[:, pl.ds(pl.multiple_of(slab * width, 128), width)],
-            contract_last,
-            preferred_element_type=f32,
-        )
-
-    scale = lax.rsqrt(square_sum[...] * (1.0 / (8 * width)) + epsilon)
-    scores = score_sum[...] * scale
-    affinity = 1.0 / (1.0 + jnp.exp(-scores))
-    experts = lax.broadcasted_iota(jnp.int32, scores.shape, 1)
-    for copy in from_marks:
-        copy.wait_recv()
-    chosen = affinity * marks[...].reshape(scores.shape).astype(f32)
-    mine = jnp.sum(jnp.where(experts == lax.axis_index("ep"), chosen, 0.0), axis=1, keepdims=True)
-    weight = route_scale * mine / jnp.sum(chosen, axis=1, keepdims=True)
-    gate = gate_sum[...] * scale
-    hidden = gate / (1.0 + jnp.exp(-gate)) * (up_sum[...] * scale) * weight
-    act[...] = hidden.astype(jnp.bfloat16)
+            rank_copies[-1].start()
+    products(other)
 
     def down(p, column_half):
         first, count = out_cols[p]
@@ -443,7 +469,7 @@
         for quarter in range(2):
             start = pl.multiple_of(column_half * (2 * unit_cols) + quarter * unit_cols + first, 128)
             quarters.append(
-                jnp.dot(act[...], wd[:, pl.ds(start, count)], preferred_element_type=jnp.float32)
+                dot(act[...].reshape(8 * slots, act.shape[3]), wd[:, pl.ds(start, count)])
                 .reshape(2, 4, 4, 2, 8, count)
             )
         both = jnp.concatenate(quarters, axis=4).astype(jnp.bfloat16)
@@ -452,71 +478,73 @@
                 for zh in range(2):
                     partial[column_half, :, zh * 2 + zl, y, :, pl.ds(first, count)] = both[zl, y, :, zh]
 
-    units = range(3)
-    to_core = []
-    for p in units:
+    rest = [tuple(a for a in AXES if a != order[2]) for order in ORDERS]
+    from_core = [{} for p in pieces]
+
+    def own(p, where):
+        return pick(partial.at[core], where, (slice(None), pl.ds(*out_cols[p])))
+
+    def landing(ref, p, where):
+        return pick(ref, where, (slice(None), pl.ds(0, out_cols[p][1])), rest[p])
+
+    def share_sum(p, name, last):
+        where, tail = {ORDERS[p][2]: last}, (slice(None), pl.ds(*out_cols[p]))
+        from_core[p][name] = copies.start(
+            pick(partial.at[other], where, tail), pick(core_partial, where, tail), sibling
+        )
+
+    def take_sum(p, name, last):
+        from_core[p][name].wait_recv()
+        where, tail = {ORDERS[p][2]: last}, (slice(None), pl.ds(*out_cols[p]))
+        mine = own(p, where)
+        mine[...] = (mine[...].astype(f32) + pick(core_partial, where, tail)[...].astype(f32)).astype(bf16)
+
+    for p in pieces:
         down(p, other)
-        cols = pl.ds(*out_cols[p])
-        to_core.append(
-            copies.start(partial.at[other, :, :, :, :, cols], core_partial.at[:, :, :, :, cols], sibling)
+        share_sum(p, "across", across[p])
+    for p in pieces:
+        share_sum(p, "after", after[p])
+        share_sum(p, "before", before[p])
+    for p in pieces:
+        share_sum(p, "here", here[p])
+    far, near_sums = [], []
+    for p, (first, second, last) in enumerate(ORDERS):
+        down(p, core)
+        take_sum(p, "across", across[p])
+        one, two = {second: pl.ds(0, 2)}, {second: pl.ds(2, 2)}
+        far.append(
+            (
+                copies.start(own(p, {last: across[p], **one}), landing(far_parts.at[p], p, one), rights[p]),
+                copies.start(own(p, {last: across[p], **two}), landing(far_parts.at[p], p, two), lefts[p]),
+            )
         )
-    rest = [tuple(a for a in AXES if a != order[2]) for order in ORDERS]
-    far, near = {}, {}
-
     for p, (first, second, last) in enumerate(ORDERS):
-        cols = pl.ds(*out_cols[p])
-        width_p = out_cols[p][1]
-        down(p, core)
-        to_core[p].wait_recv()
-
-        @pl.loop(0, 4)
-        def _(x):
-            partial[core, x, :, :, :, cols] = (
-                partial[core, x, :, :, :, cols].astype(jnp.float32)
-                + core_partial[x, :, :, :, cols].astype(jnp.float32)
-            ).astype(jnp.bfloat16)
-
-        def source(where):
-            return pick(partial.at[core], where, (slice(None), cols))
-
-        right, left = device(moved(me, last, 1), core), device(moved(me, last, 3), core)
-        before, after, across = (me[last] + 3) % 4, (me[last] + 1) % 4, (me[last] + 2) % 4
-        tail = (slice(None), pl.ds(0, width_p))
-
-        def landing(ref, where):
-            return pick(ref, where, tail, rest[p])
-
-        a, b = {second: pl.ds(0, 2)}, {second: pl.ds(2, 2)}
-        far_a = copies.start(source({last: across, **a}), landing(far_parts.at[p], a), right)
-        far_b = copies.start(source({last: across, **b}), landing(far_parts.at[p], b), left)
-        right_b = copies.start(source({last: after, **b}), landing(near_parts.at[p, 0], b), right)
-        left_a = copies.start(source({last: before, **a}), landing(near_parts.at[p, 1], a), left)
-        far[p], near[p] = (far_a, far_b), [right_b, left_a]
-
+        one, two = {second: pl.ds(0, 2)}, {second: pl.ds(2, 2)}
+        take_sum(p, "after", after[p])
+        right_b = copies.start(own(p, {last: after[p], **two}), landing(near_parts.at[p, 0], p, two), rights[p])
+        take_sum(p, "before", before[p])
+        left_a = copies.start(own(p, {last: before[p], **one}), landing(near_parts.at[p, 1], p, one), lefts[p])
+        near_sums.append([right_b, left_a])
     for p, (first, second, last) in enumerate(ORDERS):
-        cols = pl.ds(*out_cols[p])
-        width_p = out_cols[p][1]
-        right, left = device(moved(me, last, 1), core), device(moved(me, last, 3), core)
-        before, after = (me[last] + 3) % 4, (me[last] + 1) % 4
-        tail = (slice(None), pl.ds(0, width_p))
-        for side, (copy, part, at, to) in enumerate(
-            ((far[p][0], pl.ds(0, 2), after, right), (far[p][1], pl.ds(2, 2), before, left))
+        for side, (at, span, to) in enumerate(
+            ((after[p], pl.ds(0, 2), rights[p]), (before[p], pl.ds(2, 2), lefts[p]))
         ):
-            copy.wait_recv()
-            here = pick(partial.at[core], {last: at, second: part}, (slice(None), cols))
-            came = pick(far_parts.at[p], {second: part}, tail, rest[p])
-            here[...] = (here[...].astype(jnp.float32) + came[...].astype(jnp.float32)).astype(jnp.bfloat16)
-            near[p].append(copies.start(here, pick(near_parts.at[p, side], {second: part}, tail, rest[p]), to))
+            far[p][side].wait_recv()
+            mine = own(p, {last: at, second: span})
+            came = landing(far_parts.at[p], p, {second: span})
+            mine[...] = (mine[...].astype(f32) + came[...].astype(f32)).astype(bf16)
+            near_sums[p].append(copies.start(mine, landing(near_parts.at[p, side], p, {second: span}), to))
+    for p in pieces:
+        take_sum(p, "here", here[p])
 
     phase_two = {}
     for p, (first, second, last) in enumerate(ORDERS):
         cols = pl.ds(*out_cols[p])
         width_p = out_cols[p][1]
         tail = (slice(None), pl.ds(0, width_p))
-        for copy in near[p]:
+        for copy in near_sums[p]:
             copy.wait_recv()
-        here = pick(partial.at[core], {last: me[last]}, (slice(None), cols))
-        total = here[...].astype(jnp.float32)
+        total = own(p, {last: here[p]})[...].astype(f32)
         for side in range(2):
             total = total + near_parts[p, side, :, :, :, pl.ds(0, width_p)].astype(jnp.float32)
         sums_two[p, :, :, :, pl.ds(0, width_p)] = total.astype(jnp.bfloat16)
@@ -597,36 +625,35 @@
             jax.ShapeDtypeStruct((slots, model), bf16),
             jax.ShapeDtypeStruct((4, model), bf16),
         ),
-        in_specs=[vmem] * 5 + [hbm] * 8,
+        in_specs=[vmem] * 3 + [hbm] * 10,
         out_specs=(hbm, vmem),
         scratch_shapes=[
+            pltpu.VMEM(queries.shape, bf16),
+            pltpu.VMEM((4, 1, 2 * width), f32),
             pltpu.VMEM((slots * cap, latent_width), bf16),
             pltpu.VMEM((slots, rope_width, cap), bf16),
+            pltpu.VMEM((slots // 16, rope_width, 16 * cap), bf16),
             pltpu.VMEM(w_absorb.shape, bf16),
             pltpu.VMEM((heads, slots, latent_width), bf16),
             pltpu.VMEM((heads, slots, rope_width), bf16),
             pltpu.VMEM((8, 16, latent_width + 128), bf16),
             pltpu.VMEM((8, 16, latent_width + 128), bf16),
-            pltpu.VMEM((slots, experts), bf16),
-            pltpu.VMEM((8, slots, experts), bf16),
+            pltpu.VMEM((2, half, experts), bf16),
+            pltpu.VMEM((8, 2, half, experts), bf16),
             pltpu.VMEM((heads, slots, latent_width), bf16),
             pltpu.VMEM((slots, heads_width), bf16),
             pltpu.VMEM((16, heads_width), bf16),
             pltpu.VMEM((8, 16, heads_width), bf16),
             pltpu.VMEM((heads_width, model), bf16),
             pltpu.VMEM((experts, model), bf16),
-            pltpu.VMEM((8, width, hidden), bf16),
-            pltpu.VMEM((8, width, hidden), bf16),
+            pltpu.VMEM((4, 2 * width, hidden), bf16),
+            pltpu.VMEM((4, 2 * width, hidden), bf16),
             pltpu.VMEM((hidden, model), bf16),
             pltpu.VMEM((8, 2, half, width), bf16),
             pltpu.VMEM((8, half, width), bf16),
             pltpu.VMEM((7, half, width), bf16),
-            pltpu.VMEM((4, 4, 4, slots, width), bf16),
-            pltpu.VMEM((rows, hidden), f32),
-            pltpu.VMEM((rows, hidden), f32),
-            pltpu.VMEM((rows, experts), f32),
-            pltpu.VMEM((rows, 1), f32),
-            pltpu.VMEM((rows, hidden), bf16),
+            pltpu.VMEM((4, 4, 4, 2, half, width), bf16),
+            pltpu.VMEM((8, 2, half, hidden), bf16),
             pltpu.VMEM((2, 4, 4, 4, 16, unit_cols), bf16),
             pltpu.VMEM((4, 4, 4, 16, unit_cols), bf16),
             pltpu.VMEM((3, 4, 4, 16, share), bf16),
@@ -636,27 +663,27 @@
             pltpu.VMEM((3, 4, 16, share), bf16),
             pltpu.VMEM((3, 3, 16, share), bf16),
             pltpu.VMEM((2, 16, unit_cols), bf16),
-            pltpu.SemaphoreType.DMA((32,)),
-            pltpu.SemaphoreType.DMA((128,)),
-            pltpu.SemaphoreType.DMA((128,)),
+            pltpu.SemaphoreType.DMA((56,)),
+            pltpu.SemaphoreType.DMA((160,)),
+            pltpu.SemaphoreType.DMA((160,)),
         ],
         compiler_params=pltpu.CompilerParams(
             collective_id=0, has_side_effects=True, vmem_limit_bytes=60 * 1024 * 1024
         ),
         name="decode",
     )(
-        queries,
         plan,
         lengths,
         routes.T,
-        gain.reshape(8, 1, width),
+        queries,
+        gain.reshape(4, 1, 2 * width),
         cache_latent.reshape(slots * cap, latent_width),
         cache_rope.transpose(0, 2, 1),
         w_absorb,
         w_out,
         router.T,
-        w_gate.reshape(8, width, hidden),
-        w_up.reshape(8, width, hidden),
+        w_gate.reshape(4, 2 * width, hidden),
+        w_up.reshape(4, 2 * width, hidden),
         w_down,
     )
 

time: 104 us -> 101 us (0.971)
  Pallas kernels: 103 us -> 100 us
    pallas_call x1, Pallas kernels: 101 us -> 98.1 us  [run_decode(): pl.pallas_call(decode_kernel, out_shape=(jax.ShapeDtypeStruct((slots, mod...]
where the time goes in v4:
time: 101 us
  Pallas kernels  100 us (99%)
    pallas_call x1, Pallas kernels, run_decode(): pl.pallas_call(decode_kernel, out_shape=(jax.ShapeDtypeStruct((slots, mod...  98.1 us
    pallas_call x1, Pallas kernels, write_out(): pl.pallas_call(copy_kernel, out_shape=(jax.ShapeDtypeStruct(attended.shap...  2.08 us

profile of v4, /device:TPU:1, one launch (start us, length us, event | category | flops | bytes accessed | tf_op | source)
XLA Modules:
  0.0 101.0 jit_solution(14546558974480677293)
XLA Ops:
  0.6 98.1 %decode.1 = (bf16[64,7168]{1,0:T(8,128)(2,1)}, bf16[4,7168]{1,0:T(4,128)(2,1)}) custom-call(s32[1,512]{1,0:T(1,128)} %bitcast.18, s32[1,64]{1,0:T(1,128)} %bitcast.19, s32[8,64]{1,0:T(8,128)} %bitcast.17, bf16[64,2304]{1,0:T(8,128)(2,1)} %queries_in.1, f32[4,1,1792]{2,1,0:T(1,128)} %bitcast.16, bf16[5120,512]{1,0:T(8,128)(2,1)} %bitcast.10, ...), custom_call_target="tpu_custom_call" | custom-call | tf_op jit(solution)/shard_map/decode/pallas_call | solution.py:622
  98.7 2.1 %write_out.1 = (bf16[64,7168]{1,0:T(8,128)(2,1)}, bf16[4,7168]{1,0:T(4,128)(2,1)}) custom-call(bf16[64,7168]{1,0:T(8,128)(2,1)} %get-tuple-element.4.source, bf16[4,7168]{1,0:T(4,128)(2,1)} %get-tuple-element.5.small_source), custom_call_target="tpu_custom_call" | custom-call | tf_op jit(solution)/shard_map/write_out/pallas_call | solution.py:716

commit v5 on v4

--- a/solution.py
+++ b/solution.py
@@ -87,8 +87,10 @@
     marks,
     latent_out,
     values,
-    values_out,
-    values_in,
+    places,
+    logits,
+    act_source,
+    rank_rows,
     wo,
     wr,
     wg,
@@ -258,7 +260,6 @@
     marks_out[...] = named.astype(bf16).reshape(marks_out.shape)
     marks[my_rank] = marks_out[...]
     query_in[my_rank] = jnp.zeros(query_in.shape[1:], bf16)
-    values_in[my_rank] = jnp.zeros(values_in.shape[1:], bf16)
 
     pl.semaphore_wait(barrier, len(peers))
     from_ranks = []
@@ -313,19 +314,6 @@
     for h in range(heads):
         values[:, h * VDIM : (h + 1) * VDIM] = dot(latent_out[h], wa[h]).astype(bf16)
 
-    guest_column = jnp.concatenate(guest_slot, axis=0)
-    select = mark(guest_column == iota((16, slots), 1).astype(f32)).astype(bf16)
-    values_out[...] = dot(select, values[...]).astype(bf16)
-    from_ranks = []
-    for dz, dy in rank_offsets:
-        from_ranks.append(copies.start(values_out, values_in.at[my_rank], device(rank_chip(dz, dy), core)))
-    for copy in from_ranks:
-        copy.wait_recv()
-    place = (key >> 1) * 16 + (key & 1) * 8 + my_rank
-    back = mark((iota((slots, 128), 1) == place) & (key >= 0)).astype(bf16)
-    returned = dot(back, values_in[...].reshape(128, values_in.shape[2]))
-    values[...] = jnp.where(stays, values[...].astype(f32), returned).astype(bf16)
-
     from_sibling = []
     for load in loads[:8]:
         load.wait()
@@ -342,6 +330,10 @@
             from_slabs.append(
                 copies.start(terms.at[k, core], slab_terms.at[k], device(slab_chip(dx, dz), core))
             )
+    for r in range(8):
+        source = jnp.sum(jnp.where(diagonal, sources[r : r + 1, :], 0).astype(f32), axis=1, keepdims=True)
+        lanes = iota((slots, 8 * slots), 1)
+        places[r] = mark(source.astype(jnp.int32) == lanes).astype(bf16)
     for k, copy in enumerate(from_slabs):
         copy.wait_recv()
         total = total + slab_terms[k].astype(jnp.float32)
@@ -437,31 +429,29 @@
             )
 
         scale = lax.rsqrt(jnp.sum(square_sum, axis=1, keepdims=True) * (1.0 / (8 * width)) + epsilon)
-        affinity = 1.0 / (1.0 + jnp.exp(-score * scale))
-        chosen = affinity * marks[:, side].reshape(affinity.shape).astype(f32)
-        expert = iota(affinity.shape, 1)
-        mine = jnp.sum(jnp.where(expert == lax.axis_index("ep"), chosen, 0.0), axis=1, keepdims=True)
-        weight = route_scale * mine / jnp.sum(chosen, axis=1, keepdims=True)
+        score = score * scale
+        high = score.astype(bf16)
+        low = (score - high.astype(f32)).astype(bf16)
+        logits[:, side] = jnp.concatenate([high, low], axis=1).reshape(8, half, 2 * score.shape[1])
         gate = gate * scale
-        hidden = gate / (1.0 + jnp.exp(-gate)) * (up * scale) * weight
-        act[:, side] = hidden.astype(bf16).reshape(8, half, hidden.shape[1])
+        hidden = gate / (1.0 + jnp.exp(-gate)) * (up * scale)
+        act_source[:, side] = hidden.astype(bf16).reshape(8, half, hidden.shape[1])
 
     products(core)
     for copy in to_core:
         copy.wait_recv()
 
-    rank_copies = []
-    for slab in range(8):
-        for side in range(2):
-            rank_copies.append(
-                pltpu.make_async_copy(
-                    tokens.at[slab // 2, slab % 2 * 2 + me["z"] % 2, me["y"], side],
-                    attended.at[pl.ds(side * half, half), pl.ds(slab * width, width)],
-                    load_sem.at[32 + 2 * slab + side],
-                )
-            )
-            rank_copies[-1].start()
     products(other)
+
+    all_places = places[...].reshape(8 * slots, 8 * slots)
+    experts = marks.shape[3]
+    pair = dot(all_places, logits[...].reshape(8 * slots, 2 * experts))
+    affinity = 1.0 / (1.0 + jnp.exp(-(pair[:, :experts] + pair[:, experts:])))
+    chosen = affinity * marks[...].reshape(affinity.shape).astype(f32)
+    mine = jnp.where(iota(affinity.shape, 1) == lax.axis_index("ep"), chosen, 0.0)
+    weight = route_scale * jnp.sum(mine, axis=1, keepdims=True) / jnp.sum(chosen, axis=1, keepdims=True)
+    moved_act = dot(all_places, act_source[...].reshape(8 * slots, act.shape[3])) * weight
+    act[...] = moved_act.astype(bf16).reshape(act.shape)
 
     def down(p, column_half):
         first, count = out_cols[p]
@@ -525,6 +515,19 @@
         take_sum(p, "before", before[p])
         left_a = copies.start(own(p, {last: before[p], **one}), landing(near_parts.at[p, 1], p, one), lefts[p])
         near_sums.append([right_b, left_a])
+
+    rank_copies = []
+    for slab in range(8):
+        rows = tokens[slab // 2, pl.ds(slab % 2 * 2, 2)].reshape(8 * slots, width)
+        rank_rows[slab] = dot(places[my_rank], rows).astype(bf16)
+    for slab in range(8):
+        rank_copies.append(
+            pltpu.make_async_copy(
+                rank_rows.at[slab], attended.at[:, pl.ds(slab * width, width)], load_sem.at[12 + slab]
+            )
+        )
+        rank_copies[-1].start()
+
     for p, (first, second, last) in enumerate(ORDERS):
         for side, (at, span, to) in enumerate(
             ((after[p], pl.ds(0, 2), rights[p]), (before[p], pl.ds(2, 2), lefts[p]))
@@ -642,8 +645,10 @@
             pltpu.VMEM((8, 2, half, experts), bf16),
             pltpu.VMEM((heads, slots, latent_width), bf16),
             pltpu.VMEM((slots, heads_width), bf16),
-            pltpu.VMEM((16, heads_width), bf16),
-            pltpu.VMEM((8, 16, heads_width), bf16),
+            pltpu.VMEM((8, slots, rows), bf16),
+            pltpu.VMEM((8, 2, half, 2 * experts), bf16),
+            pltpu.VMEM((8, 2, half, hidden), bf16),
+            pltpu.VMEM((8, slots, width), bf16),
             pltpu.VMEM((heads_width, model), bf16),
             pltpu.VMEM((experts, model), bf16),
             pltpu.VMEM((4, 2 * width, hidden), bf16),

time: 101 us -> 96.2 us (0.952)
  Pallas kernels: 100 us -> 95.3 us
    pallas_call x1, Pallas kernels: 98.1 us -> 93.2 us  [run_decode(): pl.pallas_call(decode_kernel, out_shape=(jax.ShapeDtypeStruct((slots, mod...]
where the time goes in v5:
time: 96.2 us; the launch traced here: 96.1 us
  Pallas kernels  95.3 us (99%)
    pallas_call x1, Pallas kernels, run_decode(): pl.pallas_call(decode_kernel, out_shape=(jax.ShapeDtypeStruct((slots, mod...  93.2 us
    pallas_call x1, Pallas kernels, write_out(): pl.pallas_call(copy_kernel, out_shape=(jax.ShapeDtypeStruct(attended.shap...  2.08 us

profile of v5, /device:TPU:1, one launch (start us, length us, event | category | flops | bytes accessed | tf_op | source)
XLA Modules:
  0.0 96.1 jit_solution(5561014035030562527)
XLA Ops:
  0.6 93.2 %decode.1 = (bf16[64,7168]{1,0:T(8,128)(2,1)}, bf16[4,7168]{1,0:T(4,128)(2,1)}) custom-call(s32[1,512]{1,0:T(1,128)} %bitcast.18, s32[1,64]{1,0:T(1,128)} %bitcast.19, s32[8,64]{1,0:T(8,128)} %bitcast.17, bf16[64,2304]{1,0:T(8,128)(2,1)} %queries_in.1, f32[4,1,1792]{2,1,0:T(1,128)} %bitcast.16, bf16[5120,512]{1,0:T(8,128)(2,1)} %bitcast.10, ...), custom_call_target="tpu_custom_call" | custom-call | tf_op jit(solution)/shard_map/decode/pallas_call | solution.py:625
  93.8 2.1 %write_out.1 = (bf16[64,7168]{1,0:T(8,128)(2,1)}, bf16[4,7168]{1,0:T(4,128)(2,1)}) custom-call(bf16[64,7168]{1,0:T(8,128)(2,1)} %get-tuple-element.4.source, bf16[4,7168]{1,0:T(4,128)(2,1)} %get-tuple-element.5.small_source), custom_call_target="tpu_custom_call" | custom-call | tf_op jit(solution)/shard_map/write_out/pallas_call | solution.py:721

commit v6 on v5

--- a/solution.py
+++ b/solution.py
@@ -131,7 +131,7 @@
     share = (unit_cols // 128 * 5 + 6) // 14 * 128
     out_cols = ((0, share), (share, share), (2 * share, unit_cols - 2 * share))
 
-    slab_offsets = [(dx, dz) for dx in range(4) for dz in range(2) if (dx, dz) != (0, 0)]
+    slab_offsets = [(2, 1), (1, 1), (3, 1), (2, 0), (0, 1), (1, 0), (3, 0)]
 
     def slab_chip(dx, dz):
         return {**me, "x": (me["x"] + dx) % 4, "z": (me["z"] + 2 * dz) % 4}
@@ -308,7 +308,7 @@
         seen = (position >= 0) & (position < limit)
         scores = jnp.where(seen, scores * score_scale, -jnp.inf)
         raised = jnp.exp(scores - jnp.max(scores, axis=1, keepdims=True))
-        probs = (raised / jnp.sum(raised, axis=1, keepdims=True)).astype(bf16)
+        probs = (raised * (1.0 / jnp.sum(raised, axis=1, keepdims=True))).astype(bf16)
         latent_out[:, mine, :] = dot(probs, keys[here, :]).astype(bf16).reshape(heads, group, latent_width)
     absorb_load.wait()
     for h in range(heads):
@@ -497,24 +497,43 @@
         share_sum(p, "before", before[p])
     for p in pieces:
         share_sum(p, "here", here[p])
-    far, near_sums = [], []
-    for p, (first, second, last) in enumerate(ORDERS):
+    by_right, by_left = (2, 3), (1, 0)
+    far, sum_right, sum_left = [{} for p in pieces], [{} for p in pieces], [{} for p in pieces]
+
+    def step(p, k):
+        second = ORDERS[p][1]
+        return {second: (me[second] + k) % 4}
+
+    def part(p, last, k):
+        return own(p, {ORDERS[p][2]: last, **step(p, k)})
+
+    for p in pieces:
         down(p, core)
         take_sum(p, "across", across[p])
-        one, two = {second: pl.ds(0, 2)}, {second: pl.ds(2, 2)}
-        far.append(
-            (
-                copies.start(own(p, {last: across[p], **one}), landing(far_parts.at[p], p, one), rights[p]),
-                copies.start(own(p, {last: across[p], **two}), landing(far_parts.at[p], p, two), lefts[p]),
-            )
-        )
-    for p, (first, second, last) in enumerate(ORDERS):
-        one, two = {second: pl.ds(0, 2)}, {second: pl.ds(2, 2)}
+        for kr, kl in zip(by_right, by_left):
+            for k, to in ((kr, rights[p]), (kl, lefts[p])):
+                far[p][k] = copies.start(part(p, across[p], k), landing(far_parts.at[p], p, step(p, k)), to)
+    for p in pieces:
         take_sum(p, "after", after[p])
-        right_b = copies.start(own(p, {last: after[p], **two}), landing(near_parts.at[p, 0], p, two), rights[p])
+        for k in by_left:
+            there = landing(near_parts.at[p, 0], p, step(p, k))
+            sum_right[p][k] = copies.start(part(p, after[p], k), there, rights[p])
         take_sum(p, "before", before[p])
-        left_a = copies.start(own(p, {last: before[p], **one}), landing(near_parts.at[p, 1], p, one), lefts[p])
-        near_sums.append([right_b, left_a])
+        for k in by_right:
+            there = landing(near_parts.at[p, 1], p, step(p, k))
+            sum_left[p][k] = copies.start(part(p, before[p], k), there, lefts[p])
+    for kr, kl in zip(by_right, by_left):
+        for p in pieces:
+            for k, at, side, sums, to in (
+                (kr, after[p], 0, sum_right, rights[p]),
+                (kl, before[p], 1, sum_left, lefts[p]),
+            ):
+                far[p][k].wait_recv()
+                mine, came = part(p, at, k), landing(far_parts.at[p], p, step(p, k))
+                mine[...] = (mine[...].astype(f32) + came[...].astype(f32)).astype(bf16)
+                sums[p][k] = copies.start(mine, landing(near_parts.at[p, side], p, step(p, k)), to)
+    for p in pieces:
+        take_sum(p, "here", here[p])
 
     rank_copies = []
     for slab in range(8):
@@ -528,44 +547,27 @@
         )
         rank_copies[-1].start()
 
-    for p, (first, second, last) in enumerate(ORDERS):
-        for side, (at, span, to) in enumerate(
-            ((after[p], pl.ds(0, 2), rights[p]), (before[p], pl.ds(2, 2), lefts[p]))
-        ):
-            far[p][side].wait_recv()
-            mine = own(p, {last: at, second: span})
-            came = landing(far_parts.at[p], p, {second: span})
-            mine[...] = (mine[...].astype(f32) + came[...].astype(f32)).astype(bf16)
-            near_sums[p].append(copies.start(mine, landing(near_parts.at[p, side], p, {second: span}), to))
-    for p in pieces:
-        take_sum(p, "here", here[p])
-
-    phase_two = {}
-    for p, (first, second, last) in enumerate(ORDERS):
-        cols = pl.ds(*out_cols[p])
-        width_p = out_cols[p][1]
-        tail = (slice(None), pl.ds(0, width_p))
-        for copy in near_sums[p]:
-            copy.wait_recv()
-        total = own(p, {last: here[p]})[...].astype(f32)
-        for side in range(2):
-            total = total + near_parts[p, side, :, :, :, pl.ds(0, width_p)].astype(jnp.float32)
-        sums_two[p, :, :, :, pl.ds(0, width_p)] = total.astype(jnp.bfloat16)
-        phase_two[p] = []
-        for k in (1, 3, 2):
-            to = moved(me, second, k)
-            phase_two[p].append(
-                copies.start(
-                    pick(sums_two.at[p], {second: to[second]}, tail, rest[p]),
-                    parts_two.at[p, k - 1, :, :, pl.ds(0, width_p)],
-                    device(to, core),
+    phase_two = [{} for p in pieces]
+    for k in (2, 1, 3, 0):
+        for p in pieces:
+            sum_right[p][k].wait_recv()
+            sum_left[p][k].wait_recv()
+            total = part(p, here[p], k)[...].astype(f32)
+            for side in range(2):
+                total = total + landing(near_parts.at[p, side], p, step(p, k))[...].astype(f32)
+            result = landing(sums_two.at[p], p, step(p, k))
+            result[...] = total.astype(bf16)
+            if k != 0:
+                phase_two[p][k] = copies.start(
+                    result,
+                    parts_two.at[p, k - 1, :, :, pl.ds(0, out_cols[p][1])],
+                    device(moved(me, ORDERS[p][1], k), core),
                 )
-            )
     phase_three = {}
     for p, (first, second, last) in enumerate(ORDERS):
         width_p = out_cols[p][1]
         tail = (slice(None), pl.ds(0, width_p))
-        for copy in phase_two[p]:
+        for copy in phase_two[p].values():
             copy.wait_recv()
         total = pick(sums_two.at[p], {second: me[second]}, tail, rest[p])[...].astype(jnp.float32)
         for k in range(3):
@@ -669,8 +671,8 @@
             pltpu.VMEM((3, 3, 16, share), bf16),
             pltpu.VMEM((2, 16, unit_cols), bf16),
             pltpu.SemaphoreType.DMA((56,)),
-            pltpu.SemaphoreType.DMA((160,)),
-            pltpu.SemaphoreType.DMA((160,)),
+            pltpu.SemaphoreType.DMA((192,)),
+            pltpu.SemaphoreType.DMA((192,)),
         ],
         compiler_params=pltpu.CompilerParams(
             collective_id=0, has_side_effects=True, vmem_limit_bytes=60 * 1024 * 1024

time: 96.2 us -> 95.2 us (0.990)
  Pallas kernels: 95.3 us -> 94.2 us
    pallas_call x1, Pallas kernels: 93.2 us -> 92.1 us  [run_decode(): pl.pallas_call(decode_kernel, out_shape=(jax.ShapeDtypeStruct((slots, mod...]
where the time goes in v6:
time: 95.2 us; the launch traced here: 95 us
  Pallas kernels  94.2 us (99%)
    pallas_call x1, Pallas kernels, run_decode(): pl.pallas_call(decode_kernel, out_shape=(jax.ShapeDtypeStruct((slots, mod...  92.1 us
    pallas_call x1, Pallas kernels, write_out(): pl.pallas_call(copy_kernel, out_shape=(jax.ShapeDtypeStruct(attended.shap...  2.08 us

profile of v6, /device:TPU:1, one launch (start us, length us, event | category | flops | bytes accessed | tf_op | source)
XLA Modules:
  0.0 95.0 jit_solution(17019976030320002674)
XLA Ops:
  0.6 92.1 %decode.1 = (bf16[64,7168]{1,0:T(8,128)(2,1)}, bf16[4,7168]{1,0:T(4,128)(2,1)}) custom-call(s32[1,512]{1,0:T(1,128)} %bitcast.18, s32[1,64]{1,0:T(1,128)} %bitcast.19, s32[8,64]{1,0:T(8,128)} %bitcast.17, bf16[64,2304]{1,0:T(8,128)(2,1)} %queries_in.1, f32[4,1,1792]{2,1,0:T(1,128)} %bitcast.16, bf16[5120,512]{1,0:T(8,128)(2,1)} %bitcast.10, ...), custom_call_target="tpu_custom_call" | custom-call | tf_op jit(solution)/shard_map/decode/pallas_call | solution.py:627
  92.8 2.1 %write_out.1 = (bf16[64,7168]{1,0:T(8,128)(2,1)}, bf16[4,7168]{1,0:T(4,128)(2,1)}) custom-call(bf16[64,7168]{1,0:T(8,128)(2,1)} %get-tuple-element.4.source, bf16[4,7168]{1,0:T(4,128)(2,1)} %get-tuple-element.5.small_source), custom_call_target="tpu_custom_call" | custom-call | tf_op jit(solution)/shard_map/write_out/pallas_call | solution.py:723

commit v7 on v6

--- a/solution.py
+++ b/solution.py
@@ -214,18 +214,6 @@
     letter = jnp.sum(leaving * dot(leaving.astype(bf16), earlier), axis=0, keepdims=True)
     away = jnp.sum(leaving, axis=0, keepdims=True)
     key_row = jnp.where(away > 0.5, own_rank * 2.0 + letter, -1.0)
-    diagonal = iota((slots, slots), 0) == iota((slots, slots), 1)
-    key = jnp.sum(jnp.where(diagonal, key_row, 0.0), axis=1, keepdims=True).astype(jnp.int32)
-    stays = key < 0
-    length = jnp.sum(jnp.where(diagonal, lengths[...].astype(f32), 0.0), axis=1, keepdims=True).astype(jnp.int32)
-
-    arriving = mark((rank_of == my_rank) & (rank_row != my_rank))
-    nth = dot(arriving.astype(bf16), earlier)
-    guest_slot = []
-    for k in range(2):
-        is_kth = (arriving > 0.5) & (jnp.abs(nth - k) < 0.5)
-        guest_slot.append(jnp.sum(jnp.where(is_kth, slot_of + 1, 0).astype(f32), axis=1, keepdims=True) - 1.0)
-
     def letter_places(axis, shape):
         place = iota(shape, axis)
         inner = place & 15
@@ -252,6 +240,24 @@
         .astype(bf16)
         .reshape(8, 16, 128)
     )
+    pl.semaphore_wait(barrier, len(peers))
+    from_ranks = []
+    for dz, dy in rank_offsets:
+        chip = rank_chip(dz, dy)
+        to = device(chip, core)
+        from_ranks.append(copies.start(query_out.at[to[0]], query_in.at[my_rank], to))
+    diagonal = iota((slots, slots), 0) == iota((slots, slots), 1)
+    key = jnp.sum(jnp.where(diagonal, key_row, 0.0), axis=1, keepdims=True).astype(jnp.int32)
+    stays = key < 0
+    length = jnp.sum(jnp.where(diagonal, lengths[...].astype(f32), 0.0), axis=1, keepdims=True).astype(jnp.int32)
+
+    arriving = mark((rank_of == my_rank) & (rank_row != my_rank))
+    nth = dot(arriving.astype(bf16), earlier)
+    guest_slot = []
+    for k in range(2):
+        is_kth = (arriving > 0.5) & (jnp.abs(nth - k) < 0.5)
+        guest_slot.append(jnp.sum(jnp.where(is_kth, slot_of + 1, 0).astype(f32), axis=1, keepdims=True) - 1.0)
+
     experts = iota((slots, marks.shape[3]), 1)
     named = jnp.zeros(experts.shape, f32)
     for k in range(routes.shape[0]):
@@ -260,13 +266,6 @@
     marks_out[...] = named.astype(bf16).reshape(marks_out.shape)
     marks[my_rank] = marks_out[...]
     query_in[my_rank] = jnp.zeros(query_in.shape[1:], bf16)
-
-    pl.semaphore_wait(barrier, len(peers))
-    from_ranks = []
-    for dz, dy in rank_offsets:
-        chip = rank_chip(dz, dy)
-        to = device(chip, core)
-        from_ranks.append(copies.start(query_out.at[to[0]], query_in.at[my_rank], to))
     from_marks = []
     for dz, dy in rank_offsets:
         from_marks.append(copies.start(marks_out, marks.at[my_rank], device(rank_chip(dz, dy), core)))
@@ -412,7 +411,7 @@
     for copy in from_marks:
         copy.wait_recv()
 
-    def products(side):
+    def products(side, scored):
         square_sum = jnp.zeros((8 * half, 128), f32)
         gate, up, score = 0.0, 0.0, 0.0
         for x in range(4):
@@ -424,24 +423,28 @@
             gained = (rows * gain[x]).astype(bf16)
             gate = gate + dot(gained, wg[x])
             up = up + dot(gained, wu[x])
-            score = score + lax.dot_general(
-                gained, wr[:, x * 2 * width : (x + 1) * 2 * width], contract_last, preferred_element_type=f32
-            )
+            if scored:
+                score = score + lax.dot_general(
+                    gained, wr[:, x * 2 * width : (x + 1) * 2 * width], contract_last, preferred_element_type=f32
+                )
 
         scale = lax.rsqrt(jnp.sum(square_sum, axis=1, keepdims=True) * (1.0 / (8 * width)) + epsilon)
-        score = score * scale
-        high = score.astype(bf16)
-        low = (score - high.astype(f32)).astype(bf16)
-        logits[:, side] = jnp.concatenate([high, low], axis=1).reshape(8, half, 2 * score.shape[1])
+        if scored:
+            score = score * scale
+            high = score.astype(bf16)
+            low = (score - high.astype(f32)).astype(bf16)
+            logits[:, side] = jnp.concatenate([high, low], axis=1).reshape(8, half, 2 * score.shape[1])
         gate = gate * scale
         hidden = gate / (1.0 + jnp.exp(-gate)) * (up * scale)
         act_source[:, side] = hidden.astype(bf16).reshape(8, half, hidden.shape[1])
 
-    products(core)
+    products(core, True)
+    scores_copy = copies.start(logits.at[:, core], logits.at[:, core], sibling)
     for copy in to_core:
         copy.wait_recv()
 
-    products(other)
+    products(other, False)
+    scores_copy.wait_recv()
 
     all_places = places[...].reshape(8 * slots, 8 * slots)
     experts = marks.shape[3]

time: 95.2 us -> 96 us (level)
  no operation moved by 1% of the time
where the time goes in v7:
time: 96 us; the launch traced here: 95.8 us
  Pallas kernels  95 us (99%)
    pallas_call x1, Pallas kernels, run_decode(): pl.pallas_call(decode_kernel, out_shape=(jax.ShapeDtypeStruct((slots, mod...  93 us
    pallas_call x1, Pallas kernels, write_out(): pl.pallas_call(copy_kernel, out_shape=(jax.ShapeDtypeStruct(attended.shap...  2.08 us

profile of v7, /device:TPU:1, one launch (start us, length us, event | category | flops | bytes accessed | tf_op | source)
XLA Modules:
  0.0 95.8 jit_solution(10841408800674928263)
XLA Ops:
  0.6 93.0 %decode.1 = (bf16[64,7168]{1,0:T(8,128)(2,1)}, bf16[4,7168]{1,0:T(4,128)(2,1)}) custom-call(s32[1,512]{1,0:T(1,128)} %bitcast.18, s32[1,64]{1,0:T(1,128)} %bitcast.19, s32[8,64]{1,0:T(8,128)} %bitcast.17, bf16[64,2304]{1,0:T(8,128)(2,1)} %queries_in.1, f32[4,1,1792]{2,1,0:T(1,128)} %bitcast.16, bf16[5120,512]{1,0:T(8,128)(2,1)} %bitcast.10, ...), custom_call_target="tpu_custom_call" | custom-call | tf_op jit(solution)/shard_map/decode/pallas_call | solution.py:630
  93.6 2.1 %write_out.1 = (bf16[64,7168]{1,0:T(8,128)(2,1)}, bf16[4,7168]{1,0:T(4,128)(2,1)}) custom-call(bf16[64,7168]{1,0:T(8,128)(2,1)} %get-tuple-element.4.source, bf16[4,7168]{1,0:T(4,128)(2,1)} %get-tuple-element.5.small_source), custom_call_target="tpu_custom_call" | custom-call | tf_op jit(solution)/shard_map/write_out/pallas_call | solution.py:726
